TPU v7x, 768 devices: a whole 4x8x12 slice. The times are simulated.
768 devices in a mesh: dom: 96 (over z, x, core), mp: 8 (over y).
Axes of the slice: x: 4, y: 8, z: 12, core: 2. Of those that a mesh axis runs over, the one named last changes fastest.
Arguments:
- node_states: bfloat16 [49152, 1024], P(('dom', 'mp')), may hold values from -6 to 6
- edge_states: bfloat16 [147456, 1024], P(('dom', 'mp')), may hold values from -6 to 6
- edge_weight: bfloat16 [1024, 1024], P('mp'), may hold values from -0.109375 to 0.109375
- send_weight: bfloat16 [1024, 1024], P('mp'), may hold values from -0.109375 to 0.109375
- receive_weight: bfloat16 [1024, 1024], P('mp'), may hold values from -0.109375 to 0.109375
- output_weight: bfloat16 [1024, 1024], P('mp'), may hold values from -0.1875 to 0.1875
- norm_gain: float32 [1024], replicated, may hold values from 0.5 to 1.5
- senders: int32 [147456], P(('dom', 'mp')), may hold values from 0 to 127
- receivers: int32 [147456], P(('dom', 'mp')), may hold values from 0 to 63
- send_rows: int32 [768, 4, 16], P(('dom', 'mp')), may hold values from 0 to 63
- node_cotangent: bfloat16 [49152, 1024], P(('dom', 'mp')), may hold values from -6 to 6
- edge_cotangent: bfloat16 [147456, 1024], P(('dom', 'mp')), may hold values from -6 to 6
Outputs:
- new_nodes: bfloat16 [49152, 1024], P(('dom', 'mp'))
- new_edges: bfloat16 [147456, 1024], P(('dom', 'mp'))
- grad_nodes: bfloat16 [49152, 1024], P(('dom', 'mp'))
- grad_edges: bfloat16 [147456, 1024], P(('dom', 'mp'))
Inputs may be any that keep to these rules, and one draw needn't show every extreme that they name: `senders`: A table row of the edge's own block. `receivers`: A node of the edge's own block. `send_rows`: local node indices of the sending block; a node may be listed more than once.
All inputs are finite; a program needn't handle non-finite values.
Results may differ from a plain program's by a relative error of at most 0.0059.
Values may be sent and summed in bfloat16 or wider, within the bound.
No kernel may reach another device: no remote copies, remote signals or barrier semaphores. Data moves between devices by JAX's collectives and lax.ppermute only.
A program may use at most 32 MiB of HBM per device.

v0:
```python
import jax
import jax.numpy as jnp
from jax import lax
from jax.sharding import PartitionSpec as P

eps = 1e-05


def shifted(value, axis, steps):
    count = lax.axis_size(axis)
    pairs = [(source, (source + steps) % count) for source in range(count)]
    return lax.ppermute(value, axis, pairs)


def normalize(values, norm_gain):
    average = jnp.mean(values, axis=-1, keepdims=True)
    centred = values - average
    variance = jnp.mean(centred * centred, axis=-1, keepdims=True)
    return centred * lax.rsqrt(variance + eps) * norm_gain


def silu_slope(preact):
    sigmoid_value = jax.nn.sigmoid(preact)
    return sigmoid_value * (1.0 + preact * (1.0 - sigmoid_value))


def product(left, right):
    return jnp.dot(left, right, preferred_element_type=jnp.float32)


def rows_product(left, right):
    return lax.dot_general(
        left, right, (((1,), (1,)), ((), ())), preferred_element_type=jnp.float32
    )


def send_out(block, stride):
    return shifted(block, ("dom", "mp"), stride)


def send_back(block, stride):
    return shifted(block, ("dom", "mp"), stride)


def shards(
    node_states,
    edge_states,
    edge_weight,
    send_weight,
    receive_weight,
    output_weight,
    norm_gain,
    senders,
    receivers,
    send_rows,
    node_cotangent,
    edge_cotangent,
):
    node_count = node_states.shape[0]
    spread = send_rows.shape[1] // 2
    halo_rows = send_rows.shape[2]
    shifts = [stride + 1 for stride in range(spread)] + [-(stride + 1) for stride in range(spread)]
    chosen_rows = send_rows[0]

    def collect(source):
        arrived = [
            send_out(jnp.take(source, chosen_rows[block_index], axis=0), shifts[block_index])
            for block_index in range(2 * spread)
        ]
        return jnp.concatenate([source] + arrived, axis=0)

    output_full = lax.all_gather(output_weight, "mp", axis=0, tiled=True)
    edge_full, send_full, receive_full = (
        lax.all_gather(edge_weight, "mp", axis=0, tiled=True),
        lax.all_gather(send_weight, "mp", axis=0, tiled=True),
        lax.all_gather(receive_weight, "mp", axis=0, tiled=True),
    )
    edge_part = product(edge_states, edge_full)
    send_projection = product(node_states, send_full)
    receive_projection = product(node_states, receive_full)
    send_projection = send_projection.astype(jnp.bfloat16)
    receive_projection = receive_projection.astype(jnp.bfloat16)
    lookup = collect(send_projection)
    preact = edge_part + jnp.take(lookup, senders, axis=0).astype(jnp.float32)
    preact = preact + jnp.take(receive_projection, receivers, axis=0).astype(jnp.float32)
    hidden = jax.nn.silu(preact).astype(jnp.bfloat16)
    projected = product(hidden, output_full)

    def apply_norm(values):
        return normalize(values, norm_gain)

    update, norm_back = jax.vjp(apply_norm, projected)
    new_edges = (edge_states.astype(jnp.float32) + update).astype(jnp.bfloat16)
    summed = jax.ops.segment_sum(new_edges.astype(jnp.float32), receivers, num_segments=node_count)
    new_nodes = (node_states.astype(jnp.float32) + summed).astype(jnp.bfloat16)
    grad_total = edge_cotangent.astype(jnp.float32) + jnp.take(
        node_cotangent, receivers, axis=0
    ).astype(jnp.float32)
    grad_projected = norm_back(grad_total)[0].astype(jnp.bfloat16)
    grad_hidden = rows_product(grad_projected, output_full)
    grad_preact = (grad_hidden * silu_slope(preact)).astype(jnp.bfloat16)
    grad_lookup = jax.ops.segment_sum(
        grad_preact.astype(jnp.float32), senders, num_segments=lookup.shape[0]
    )
    grad_receive = jax.ops.segment_sum(
        grad_preact.astype(jnp.float32), receivers, num_segments=node_count
    ).astype(jnp.bfloat16)
    grad_send = grad_lookup[:node_count]
    for block_index in range(2 * spread):
        start_row = node_count + block_index * halo_rows
        returned = send_back(
            grad_lookup[start_row : start_row + halo_rows].astype(jnp.bfloat16),
            -shifts[block_index],
        )
        grad_send = grad_send.at[chosen_rows[block_index]].add(returned.astype(jnp.float32))
    grad_send = grad_send.astype(jnp.bfloat16)
    grad_edge_part = rows_product(grad_preact, edge_full)
    grad_node_part = rows_product(grad_send, send_full) + rows_product(grad_receive, receive_full)
    grad_edges = (grad_total + grad_edge_part).astype(jnp.bfloat16)
    grad_nodes = (node_cotangent.astype(jnp.float32) + grad_node_part).astype(jnp.bfloat16)
    return (new_nodes, new_edges, grad_nodes, grad_edges)


def solution(mesh):
    in_specs = (
        P(("dom", "mp"), None),
        P(("dom", "mp"), None),
        P("mp", None),
        P("mp", None),
        P("mp", None),
        P("mp", None),
        P(),
        P(("dom", "mp")),
        P(("dom", "mp")),
        P(("dom", "mp"), None, None),
        P(("dom", "mp"), None),
        P(("dom", "mp"), None),
    )
    out_specs = (
        P(("dom", "mp"), None),
        P(("dom", "mp"), None),
        P(("dom", "mp"), None),
        P(("dom", "mp"), None),
    )
    return jax.shard_map(shards, mesh=mesh, in_specs=in_specs, out_specs=out_specs, check_vma=False)
```

profile of v0, /device:TPU:10, one launch (start us, length us, event | category | flops | bytes accessed | tf_op | source)
XLA Modules:
  0.0 259.3 jit_solution(7049007171523913239)
XLA Ops:
  14.8 48.3 %all-gather.7.cloned.1.call-done = bf16[1024,1024]{1,0:T(8,128)(2,1)} async-done(((bf16[128,1024]{1,0:T(8,128)(2,1)}), bf16[1024,1024]{1,0:T(8,128)(2,1)}) %all-gather.7.cloned.1.call-update) | async-done | bytes 2097168 | tf_op jit(solution)/shard_map/all_gather | solution.py:75
  63.1 2.1 constant_dynamic-update-slice_fusion.4
  65.9 2.7 %collective-permute-start = (bf16[16,1024]{1,0:T(8,128)(2,1)S(1)}, bf16[16,1024]{1,0:T(8,128)(2,1)S(1)}, u32[]{:S(2)}, u32[]{:S(2)}) collective-permute-start(bf16[16,1024]{1,0:T(8,128)(2,1)S(1)} %broadcast_select_fusion.4), channel_id=1, source_target_pairs={{0,1},{1,2},{2,3},{3,4},{4,5},{5,6},{6,7},{7,8},{8,9},{9,10},{10,1... | collective-permute-start | bytes 98312 | tf_op jit(solution)/shard_map/ppermute | solution.py:12
  69.2 4.3 %collective-permute-start.1 = (bf16[16,1024]{1,0:T(8,128)(2,1)S(1)}, bf16[16,1024]{1,0:T(8,128)(2,1)S(1)}, u32[]{:S(2)}, u32[]{:S(2)}) collective-permute-start(bf16[16,1024]{1,0:T(8,128)(2,1)S(1)} %broadcast_select_fusion.3), channel_id=1, source_target_pairs={{0,2},{1,3},{2,4},{3,5},{4,6},{5,7},{6,8},{7,9},{8,10},{9,11},{10,... | collective-permute-start | bytes 98312 | tf_op jit(solution)/shard_map/ppermute | solution.py:12
  74.2 2.8 %collective-permute-start.2 = (bf16[16,1024]{1,0:T(8,128)(2,1)S(1)}, bf16[16,1024]{1,0:T(8,128)(2,1)S(1)}, u32[]{:S(2)}, u32[]{:S(2)}) collective-permute-start(bf16[16,1024]{1,0:T(8,128)(2,1)S(1)} %broadcast_select_fusion.2), channel_id=1, source_target_pairs={{0,767},{1,0},{2,1},{3,2},{4,3},{5,4},{6,5},{7,6},{8,7},{9,8},{10,... | collective-permute-start | bytes 98312 | tf_op jit(solution)/shard_map/ppermute | solution.py:12
  77.7 4.3 %collective-permute-start.3 = (bf16[16,1024]{1,0:T(8,128)(2,1)S(1)}, bf16[16,1024]{1,0:T(8,128)(2,1)S(1)}, u32[]{:S(2)}, u32[]{:S(2)}) collective-permute-start(bf16[16,1024]{1,0:T(8,128)(2,1)S(1)} %broadcast_select_fusion.1), channel_id=1, source_target_pairs={{0,766},{1,767},{2,0},{3,1},{4,2},{5,3},{6,4},{7,5},{8,6},{9,7},{1... | collective-permute-start | bytes 98312 | tf_op jit(solution)/shard_map/ppermute | solution.py:12
  82.0 29.0 %all-gather.5.cloned.1.call-done = bf16[1024,1024]{1,0:T(8,128)(2,1)} async-done(((bf16[128,1024]{1,0:T(8,128)(2,1)}), bf16[1024,1024]{1,0:T(8,128)(2,1)}) %all-gather.5.cloned.1.call-update) | async-done | bytes 2097168 | tf_op jit(solution)/shard_map/all_gather | solution.py:74
  111.0 2.2 fusion.36
  113.2 45.9 %all-gather.9.cloned.1.call-done = bf16[1024,1024]{1,0:T(8,128)(2,1)} async-done(((bf16[128,1024]{1,0:T(8,128)(2,1)}), bf16[1024,1024]{1,0:T(8,128)(2,1)}) %all-gather.9.cloned.1.call-update) | async-done | bytes 2097168 | tf_op jit(solution)/shard_map/all_gather | solution.py:76
  159.1 2.1 convolution_convert_fusion
  163.4 43.5 %all-gather.11.cloned.1.call-done = bf16[1024,1024]{1,0:T(8,128)(2,1)} async-done(((bf16[128,1024]{1,0:T(8,128)(2,1)}), bf16[1024,1024]{1,0:T(8,128)(2,1)}) %all-gather.11.cloned.1.call-update) | async-done | bytes 2097168 | tf_op jit(solution)/shard_map/all_gather | solution.py:72
  206.9 2.5 fusion.35
  212.3 2.3 scatter_custom_fusion.1
  214.6 2.8 %scatter_custom_fusion.6 = f32[64,1024]{1,0:T(8,128)} fusion(s32[192]{0:T(256)S(1)} %copy-done.18, bf16[192,1024]{1,0:T(8,128)(2,1)S(1)} %fusion, f32[]{:T(128)} %constant.36.clone.1), kind=kCustom, calls=%fused_computation.24 | custom fusion | flops 393216 | bytes 655364 | tf_op jit(solution)/shard_map/scatter-add | solution.py:105
  218.2 2.7 %collective-permute-start.4 = (bf16[16,1024]{1,0:T(8,128)(2,1)}, bf16[16,1024]{1,0:T(8,128)(2,1)}, u32[]{:S(2)}, u32[]{:S(2)}) collective-permute-start(bf16[16,1024]{1,0:T(8,128)(2,1)} %get-tuple-element.22), channel_id=1, source_target_pairs={{0,767},{1,0},{2,1},{3,2},{4,3},{5,4},{6,5},{7,6},{8,7},{9,8},{10,... | collective-permute-start | bytes 98312 | tf_op jit(solution)/shard_map/ppermute | solution.py:12
  222.8 3.4 %collective-permute-start.6 = (bf16[16,1024]{1,0:T(8,128)(2,1)}, bf16[16,1024]{1,0:T(8,128)(2,1)}, u32[]{:S(2)}, u32[]{:S(2)}) collective-permute-start(bf16[16,1024]{1,0:T(8,128)(2,1)} %get-tuple-element.20), channel_id=1, source_target_pairs={{0,1},{1,2},{2,3},{3,4},{4,5},{5,6},{6,7},{7,8},{8,9},{9,10},{10,1... | collective-permute-start | bytes 98312 | tf_op jit(solution)/shard_map/ppermute | solution.py:12
  226.2 5.9 %collective-permute-start.7 = (bf16[16,1024]{1,0:T(8,128)(2,1)}, bf16[16,1024]{1,0:T(8,128)(2,1)}, u32[]{:S(2)}, u32[]{:S(2)}) collective-permute-start(bf16[16,1024]{1,0:T(8,128)(2,1)} %get-tuple-element.19), channel_id=1, source_target_pairs={{0,2},{1,3},{2,4},{3,5},{4,6},{5,7},{6,8},{7,9},{8,10},{9,11},{10,... | collective-permute-start | bytes 98312 | tf_op jit(solution)/shard_map/ppermute | solution.py:12
  232.1 2.6 %fusion.1 = bf16[192,1024]{1,0:T(8,128)(2,1)} fusion(bf16[192,1024]{1,0:T(8,128)(2,1)S(1)} %fusion, bf16[1024,1024]{1,0:T(8,128)(2,1)S(1)} %copy-done.3, bf16[192,1024]{1,0:T(8,128)(2,1)} %param.27, bf16[192,1024]{1,0:T(8,128)(2,1)S(1)} %gather_fusion.6, pred[192]{0:T(512)(128)(4,1)S(1)} %compare_and_fusion), kind=kOutput, calls=%fused_computation.17 | convolution fusion | flops 403832832 | bytes 3670208 | tf_op jit(solution)/shard_map/dot_general | solution.py:32
  237.0 2.5 scatter_custom_fusion
  240.1 2.6 scatter_custom_fusion.2
  242.7 2.6 scatter_custom_fusion.3
  245.2 2.6 scatter_custom_fusion.4
  247.8 2.6 scatter_custom_fusion.5
  250.4 2.4 fusion.3
  (95 shorter events, 20.6 us)
Async XLA Ops:
  7.2 5.9 %copy-start = (bf16[64,1024]{1,0:T(8,128)(2,1)S(1)}, bf16[64,1024]{1,0:T(8,128)(2,1)}, u32[]{:S(2)}) copy-start(bf16[64,1024]{1,0:T(8,128)(2,1)} %param.26) | copy-start | bytes 393220
  7.2 56.0 %all-gather.7.cloned.1.call-start = ((), (), s32[]{:S(2)}) async-start(), calls=%async_computation.1 | async-start | bytes 2359296 | tf_op jit(solution)/shard_map/all_gather | solution.py:75
  7.9 103.1 %all-gather.5.cloned.1.call-start = ((), (), s32[]{:S(2)}) async-start(), calls=%async_computation | async-start | bytes 2359296 | tf_op jit(solution)/shard_map/all_gather | solution.py:74
  8.7 150.4 %all-gather.9.cloned.1.call-start = ((), (), s32[]{:S(2)}) async-start(), calls=%async_computation.2 | async-start | bytes 2359296 | tf_op jit(solution)/shard_map/all_gather | solution.py:76
  9.4 53.7 %copy-start.7 = (bf16[64,1024]{1,0:T(8,128)(2,1)S(1)}, bf16[64,1024]{1,0:T(8,128)(2,1)}, u32[]{:S(2)}) copy-start(bf16[64,1024]{1,0:T(8,128)(2,1)} %param.16) | copy-start | bytes 393220
  9.4 197.4 %all-gather.11.cloned.1.call-start = ((), (), s32[]{:S(2)}) async-start(), calls=%async_computation.3 | async-start | bytes 2359296 | tf_op jit(solution)/shard_map/all_gather | solution.py:72
  14.1 97.0 %copy-start.4 = (bf16[192,1024]{1,0:T(8,128)(2,1)S(1)}, bf16[192,1024]{1,0:T(8,128)(2,1)}, u32[]{:S(2)}) copy-start(bf16[192,1024]{1,0:T(8,128)(2,1)} %param.17) | copy-start | bytes 1179652
  65.9 96.3 %collective-permute-start = (bf16[16,1024]{1,0:T(8,128)(2,1)S(1)}, bf16[16,1024]{1,0:T(8,128)(2,1)S(1)}, u32[]{:S(2)}, u32[]{:S(2)}) collective-permute-start(bf16[16,1024]{1,0:T(8,128)(2,1)S(1)} %broadcast_select_fusion.4), channel_id=1, source_target_pairs={{0,1},{1,2},{2,3},{3,4},{4,5},{5,6},{6,7},{7,8},{8,9},{9,10},{10,1... | collective-permute-start | bytes 98312 | tf_op jit(solution)/shard_map/ppermute | solution.py:12
  69.2 93.0 %collective-permute-start.1 = (bf16[16,1024]{1,0:T(8,128)(2,1)S(1)}, bf16[16,1024]{1,0:T(8,128)(2,1)S(1)}, u32[]{:S(2)}, u32[]{:S(2)}) collective-permute-start(bf16[16,1024]{1,0:T(8,128)(2,1)S(1)} %broadcast_select_fusion.3), channel_id=1, source_target_pairs={{0,2},{1,3},{2,4},{3,5},{4,6},{5,7},{6,8},{7,9},{8,10},{9,11},{10,... | collective-permute-start | bytes 98312 | tf_op jit(solution)/shard_map/ppermute | solution.py:12
  74.2 88.1 %collective-permute-start.2 = (bf16[16,1024]{1,0:T(8,128)(2,1)S(1)}, bf16[16,1024]{1,0:T(8,128)(2,1)S(1)}, u32[]{:S(2)}, u32[]{:S(2)}) collective-permute-start(bf16[16,1024]{1,0:T(8,128)(2,1)S(1)} %broadcast_select_fusion.2), channel_id=1, source_target_pairs={{0,767},{1,0},{2,1},{3,2},{4,3},{5,4},{6,5},{7,6},{8,7},{9,8},{10,... | collective-permute-start | bytes 98312 | tf_op jit(solution)/shard_map/ppermute | solution.py:12
  77.7 84.6 %collective-permute-start.3 = (bf16[16,1024]{1,0:T(8,128)(2,1)S(1)}, bf16[16,1024]{1,0:T(8,128)(2,1)S(1)}, u32[]{:S(2)}, u32[]{:S(2)}) collective-permute-start(bf16[16,1024]{1,0:T(8,128)(2,1)S(1)} %broadcast_select_fusion.1), channel_id=1, source_target_pairs={{0,766},{1,767},{2,0},{3,1},{4,2},{5,3},{6,4},{7,5},{8,6},{9,7},{1... | collective-permute-start | bytes 98312 | tf_op jit(solution)/shard_map/ppermute | solution.py:12
  162.2 47.1 %copy-start.11 = (bf16[192,1024]{1,0:T(8,128)(2,1)}, bf16[192,1024]{1,0:T(8,128)(2,1)S(1)}, u32[]{:S(2)}) copy-start(bf16[192,1024]{1,0:T(8,128)(2,1)S(1)} %gather_fusion.5) | copy-start | bytes 1179652
  163.3 46.0 %copy-start.13 = (bf16[192,1024]{1,0:T(8,128)(2,1)}, bf16[192,1024]{1,0:T(8,128)(2,1)S(1)}, u32[]{:S(2)}) copy-start(bf16[192,1024]{1,0:T(8,128)(2,1)S(1)} %gather_fusion) | copy-start | bytes 1179652
  163.3 46.0 %copy-start.6 = (bf16[192,1024]{1,0:T(8,128)(2,1)S(1)}, bf16[192,1024]{1,0:T(8,128)(2,1)}, u32[]{:S(2)}) copy-start(bf16[192,1024]{1,0:T(8,128)(2,1)} %param.27) | copy-start | bytes 1179652
  163.3 46.0 %copy-start.15 = (f32[1024]{0:T(1024)S(1)}, f32[1024]{0:T(1024)}, u32[]{:S(2)}) copy-start(f32[1024]{0:T(1024)} %param.22) | copy-start | bytes 12292
  212.3 19.8 %copy-start.3 = (bf16[1024,1024]{1,0:T(8,128)(2,1)S(1)}, bf16[1024,1024]{1,0:T(8,128)(2,1)}, u32[]{:S(2)}) copy-start(bf16[1024,1024]{1,0:T(8,128)(2,1)} %all-gather.5.cloned.1.call-done) | copy-start | bytes 6291460
  217.5 17.2 %copy-start.1 = (bf16[1024,1024]{1,0:T(8,128)(2,1)S(1)}, bf16[1024,1024]{1,0:T(8,128)(2,1)}, u32[]{:S(2)}) copy-start(bf16[1024,1024]{1,0:T(8,128)(2,1)} %all-gather.9.cloned.1.call-done) | copy-start | bytes 6291460
  217.5 17.2 %copy-start.8 = (f32[64,1024]{1,0:T(8,128)S(1)}, f32[64,1024]{1,0:T(8,128)}, u32[]{:S(2)}) copy-start(f32[64,1024]{1,0:T(8,128)} %scatter_custom_fusion.6) | copy-start | bytes 786436
  218.2 22.0 %collective-permute-start.4 = (bf16[16,1024]{1,0:T(8,128)(2,1)}, bf16[16,1024]{1,0:T(8,128)(2,1)}, u32[]{:S(2)}, u32[]{:S(2)}) collective-permute-start(bf16[16,1024]{1,0:T(8,128)(2,1)} %get-tuple-element.22), channel_id=1, source_target_pairs={{0,767},{1,0},{2,1},{3,2},{4,3},{5,4},{6,5},{7,6},{8,7},{9,8},{10,... | collective-permute-start | bytes 98312 | tf_op jit(solution)/shard_map/ppermute | solution.py:12
  220.9 21.8 %collective-permute-start.5 = (bf16[16,1024]{1,0:T(8,128)(2,1)}, bf16[16,1024]{1,0:T(8,128)(2,1)}, u32[]{:S(2)}, u32[]{:S(2)}) collective-permute-start(bf16[16,1024]{1,0:T(8,128)(2,1)} %get-tuple-element.21), channel_id=1, source_target_pairs={{0,766},{1,767},{2,0},{3,1},{4,2},{5,3},{6,4},{7,5},{8,6},{9,7},{1... | collective-permute-start | bytes 98312 | tf_op jit(solution)/shard_map/ppermute | solution.py:12
  222.8 22.4 %collective-permute-start.6 = (bf16[16,1024]{1,0:T(8,128)(2,1)}, bf16[16,1024]{1,0:T(8,128)(2,1)}, u32[]{:S(2)}, u32[]{:S(2)}) collective-permute-start(bf16[16,1024]{1,0:T(8,128)(2,1)} %get-tuple-element.20), channel_id=1, source_target_pairs={{0,1},{1,2},{2,3},{3,4},{4,5},{5,6},{6,7},{7,8},{8,9},{9,10},{10,1... | collective-permute-start | bytes 98312 | tf_op jit(solution)/shard_map/ppermute | solution.py:12
  226.2 21.6 %collective-permute-start.7 = (bf16[16,1024]{1,0:T(8,128)(2,1)}, bf16[16,1024]{1,0:T(8,128)(2,1)}, u32[]{:S(2)}, u32[]{:S(2)}) collective-permute-start(bf16[16,1024]{1,0:T(8,128)(2,1)} %get-tuple-element.19), channel_id=1, source_target_pairs={{0,2},{1,3},{2,4},{3,5},{4,6},{5,7},{6,8},{7,9},{8,10},{9,11},{10,... | collective-permute-start | bytes 98312 | tf_op jit(solution)/shard_map/ppermute | solution.py:12
  234.7 15.6 %copy-start.2 = (bf16[1024,1024]{1,0:T(8,128)(2,1)S(1)}, bf16[1024,1024]{1,0:T(8,128)(2,1)}, u32[]{:S(2)}) copy-start(bf16[1024,1024]{1,0:T(8,128)(2,1)} %all-gather.7.cloned.1.call-done) | copy-start | bytes 6291460
  236.9 13.4 %copy-start.10 = (f32[64,1024]{1,0:T(8,128)S(1)}, f32[64,1024]{1,0:T(8,128)}, u32[]{:S(2)}) copy-start(f32[64,1024]{1,0:T(8,128)} %fusion.15) | copy-start | bytes 786436
  (8 other events, 24.1 us)
Sparse Core Ops, SparseCore 0:
  10.4 52.7 all-gather.6
  65.5 45.4 all-gather.4
  113.4 45.6 all-gather.8
  161.3 45.4 all-gather.10
where the time goes:
time: 260 us; the launch traced here: 259 us
  waiting for transfers between devices  169 us (65%)
  starting transfers between devices  28.2 us (11%)
  other arithmetic  24.3 us (9%)
  matrix products  16.3 us (6%)
  between operations  14.2 us (5%)
  local copies, waits for them, and re-layouts  6.97 us (3%)
    all_gather x1, waiting for transfers between devices, shards(): lax.all_gather(send_weight, 'mp', axis=0, tiled=True)  48.3 us
    all_gather x1, waiting for transfers between devices, shards(): lax.all_gather(receive_weight, 'mp', axis=0, tiled=True)  45.9 us
    all_gather x1, waiting for transfers between devices, shards(): output_full = lax.all_gather(output_weight, 'mp', axis=0, tiled=True)  43.5 us
    all_gather x1, waiting for transfers between devices, shards(): lax.all_gather(edge_weight, 'mp', axis=0, tiled=True)  29 us
    ppermute x8, starting transfers between devices, shifted(): return lax.ppermute(value, axis, pairs)  28 us
    scatter-add x4, other arithmetic, shards(): grad_send.at[chosen_rows[block_index]].add(returned.astype(jnp.float32))  10.2 us
    dot_general x4, matrix products, product(): return jnp.dot(left, right, preferred_element_type=jnp.float32)  8.76 us
    dot_general x4, matrix products, rows_product(): lax.dot_general(left, right, (((1,), (1,)), ((), ())), preferred_element_...  7.51 us
  transfers between devices with their start and end apart: 12, of which 4 were waited for; matrix products, arithmetic and copies ran while one was open for 12% of the time, Pallas kernels for 0%

commit v1 on v0

v1 whole, which is shorter than its diff:
```python
import jax
import jax.numpy as jnp
from jax import lax
from jax.experimental import pallas as pl
from jax.experimental.pallas import tpu as pltpu
from jax.sharding import Mesh, PartitionSpec as P

eps = 1e-05
BF = jnp.bfloat16
F32 = jnp.float32
AXES = ("rest", "core", "mp")
EDGE, SEND, RECEIVE, OUTPUT = 0, 1, 2, 3
VMEM_BYTES = 48 * 1024 * 1024


def dot(left, right):
    return jnp.dot(left, right, preferred_element_type=F32)


def dot_rows(left, right):
    return lax.dot_general(left, right, (((1,), (1,)), ((), ())), preferred_element_type=F32)


def fetches(panels, held, sems, which):
    return [
        pltpu.make_async_copy(panels.at[core, :, which], held.at[:, core], sems.at[core])
        for core in range(2)
    ]


def begin(copies):
    for copy in copies:
        copy.start()


def finish(copies):
    for copy in copies:
        copy.wait()


def matrix(held):
    value = held[...]
    return value.reshape(-1, value.shape[-1])


def one_hot(ids_column, count):
    rows = ids_column.shape[0]
    return (lax.broadcasted_iota(jnp.int32, (rows, count), 1) == ids_column).astype(F32).astype(BF)


def one_hot_t(ids_row, count):
    columns = ids_row.shape[1]
    return (lax.broadcasted_iota(jnp.int32, (count, columns), 0) == ids_row).astype(F32).astype(BF)


def edge_kernel(
    panels, nodes, halo, edges, gain, send_col, recv_col, send_row, recv_row, node_cot, edge_cot,
    new_edges, grad_pre, own, halo_grad, grad_recv,
    w_send, w_recv, w_edge, w_out, sems,
):
    order = ((w_send, SEND), (w_recv, RECEIVE), (w_edge, EDGE), (w_out, OUTPUT))
    copies = [fetches(panels, held, sems.at[i], which) for i, (held, which) in enumerate(order)]
    for pair in copies:
        begin(pair)
    node_count = nodes.shape[0]
    table = node_count + halo.shape[0]
    pick_recv = one_hot(recv_col[...], node_count)
    grad_total = edge_cot[...].astype(F32) + dot(pick_recv, node_cot[...])
    finish(copies[0])
    lookup = dot(jnp.concatenate([nodes[...], halo[...]], axis=0), matrix(w_send)).astype(BF)
    finish(copies[1])
    received = dot(nodes[...], matrix(w_recv)).astype(BF)
    finish(copies[2])
    preact = dot(edges[...], matrix(w_edge))
    preact = preact + dot(one_hot(send_col[...], table), lookup)
    preact = preact + dot(pick_recv, received)
    gate = 1.0 / (1.0 + jnp.exp(-preact))
    hidden = (preact * gate).astype(BF)
    slope = gate * (1.0 + preact * (1.0 - gate))
    finish(copies[3])
    projected = dot(hidden, matrix(w_out))
    centred = projected - jnp.mean(projected, axis=-1, keepdims=True)
    scale = lax.rsqrt(jnp.mean(centred * centred, axis=-1, keepdims=True) + eps)
    normal = centred * scale
    new_edges[...] = (edges[...].astype(F32) + normal * gain[...]).astype(BF)
    pulled = grad_total * gain[...]
    mean_pulled = jnp.mean(pulled, axis=-1, keepdims=True)
    mean_along = jnp.mean(pulled * normal, axis=-1, keepdims=True)
    grad_projected = (scale * (pulled - mean_pulled - normal * mean_along)).astype(BF)
    grad_preact = (dot_rows(grad_projected, matrix(w_out)) * slope).astype(BF)
    grad_pre[...] = grad_preact
    grad_lookup = dot(one_hot_t(send_row[...], table), grad_preact)
    own[...] = grad_lookup[:node_count]
    halo_grad[...] = grad_lookup[node_count:].astype(BF)
    grad_recv[...] = dot(one_hot_t(recv_row[...], node_count), grad_preact).astype(BF)


def local_kernel(
    panels, nodes, new_edges, grad_pre, grad_recv, recv_col, recv_row, node_cot, edge_cot,
    new_nodes, grad_edges, part, w_edge, w_recv, sems,
):
    copies = [fetches(panels, w_edge, sems.at[0], EDGE), fetches(panels, w_recv, sems.at[1], RECEIVE)]
    for pair in copies:
        begin(pair)
    node_count = nodes.shape[0]
    summed = dot(one_hot_t(recv_row[...], node_count), new_edges[...])
    new_nodes[...] = (nodes[...].astype(F32) + summed).astype(BF)
    grad_total = edge_cot[...].astype(F32) + dot(one_hot(recv_col[...], node_count), node_cot[...])
    finish(copies[0])
    grad_edges[...] = (grad_total + dot_rows(grad_pre[...], matrix(w_edge))).astype(BF)
    finish(copies[1])
    part[...] = node_cot[...].astype(F32) + dot_rows(grad_recv[...], matrix(w_recv))


def node_kernel(panels, own, part, back_0, back_1, back_2, back_3, rows_row, grad_nodes, w_send, sems):
    copies = fetches(panels, w_send, sems, SEND)
    begin(copies)
    returned = jnp.concatenate([back_0[...], back_1[...], back_2[...], back_3[...]], axis=0)
    placed = dot(one_hot_t(rows_row[...], own.shape[0]), returned)
    grad_send = (own[...] + placed).astype(BF)
    finish(copies)
    grad_nodes[...] = (part[...] + dot_rows(grad_send, matrix(w_send))).astype(BF)


def run(kernel, outs, scratch, flops, panels, *values):
    return pl.pallas_call(
        kernel,
        out_shape=outs,
        in_specs=[pl.BlockSpec(memory_space=pl.ANY)]
        + [pl.BlockSpec(memory_space=pltpu.VMEM)] * len(values),
        out_specs=jax.tree.map(lambda _: pl.BlockSpec(memory_space=pltpu.VMEM), outs),
        scratch_shapes=scratch,
        compiler_params=pltpu.CompilerParams(vmem_limit_bytes=VMEM_BYTES),
        cost_estimate=pl.CostEstimate(flops=flops, bytes_accessed=8 * 2**20, transcendentals=0),
    )(panels, *values)


def shards(
    node_states,
    edge_states,
    edge_weight,
    send_weight,
    receive_weight,
    output_weight,
    norm_gain,
    senders,
    receivers,
    send_rows,
    node_cotangent,
    edge_cotangent,
):
    nodes, width = node_states.shape
    edges = edge_states.shape[0]
    spread, halo = send_rows.shape[1] // 2, send_rows.shape[2]
    shifts = [step + 1 for step in range(spread)] + [-(step + 1) for step in range(spread)]
    blocks = lax.axis_size(AXES)
    groups = lax.axis_size("mp")
    panel = edge_weight.shape[0] // 2
    core = lax.axis_index("core")

    def moved(value, steps):
        return lax.ppermute(value, AXES, [(i, (i + steps) % blocks) for i in range(blocks)])

    weights = jnp.stack([edge_weight, send_weight, receive_weight, output_weight])
    mine = lax.dynamic_slice_in_dim(weights, core * panel, panel, axis=1)
    gathered = lax.all_gather(mine.reshape(4 * panel, -1), ("core", "mp"), axis=0, tiled=True)
    panels = gathered.reshape(2, groups, 4, panel, -1)
    chosen = node_states.at[send_rows.reshape(-1)].get(mode="promise_in_bounds")
    arrived = [moved(chosen[j * halo : (j + 1) * halo], shifts[j]) for j in range(2 * spread)]
    halo_nodes = jnp.concatenate(arrived, axis=0)
    gain = norm_gain.reshape(1, -1)
    send_col, send_row = senders.reshape(-1, 1), senders.reshape(1, -1)
    recv_col, recv_row = receivers.reshape(-1, 1), receivers.reshape(1, -1)
    held = pltpu.VMEM((groups, 2, panel, width), BF)

    def rows(count, kind=BF):
        return jax.ShapeDtypeStruct((count, width), kind)

    new_edges, grad_pre, own, halo_grad, grad_recv = run(
        edge_kernel,
        (rows(edges), rows(edges), rows(nodes, F32), rows(2 * spread * halo), rows(nodes)),
        [held, held, held, held, pltpu.SemaphoreType.DMA((4, 2))],
        2 * 768 * width * width,
        panels, node_states, halo_nodes, edge_states, gain, send_col, recv_col, send_row, recv_row,
        node_cotangent, edge_cotangent,
    )
    back = [moved(halo_grad[j * halo : (j + 1) * halo], -shifts[j]) for j in range(2 * spread)]
    new_nodes, grad_edges, part = run(
        local_kernel,
        (rows(nodes), rows(edges), rows(nodes, F32)),
        [held, held, pltpu.SemaphoreType.DMA((2, 2))],
        2 * 256 * width * width,
        panels, node_states, new_edges, grad_pre, grad_recv, recv_col, recv_row, node_cotangent, edge_cotangent,
    )
    grad_nodes = run(
        node_kernel,
        rows(nodes),
        [held, pltpu.SemaphoreType.DMA((2,))],
        2 * 64 * width * width,
        panels, own, part, *back, send_rows.reshape(1, -1),
    )
    return new_nodes, new_edges, grad_nodes, grad_edges


def solution(mesh):
    split = Mesh(mesh.devices.reshape(-1, 2, mesh.shape["mp"]), AXES)
    rows_spec, panel_spec = P(AXES, None), P("mp", None)
    in_specs = (
        rows_spec,
        rows_spec,
        panel_spec,
        panel_spec,
        panel_spec,
        panel_spec,
        P(),
        P(AXES),
        P(AXES),
        P(AXES, None, None),
        rows_spec,
        rows_spec,
    )
    return jax.shard_map(
        shards, mesh=split, in_specs=in_specs, out_specs=(rows_spec,) * 4, check_vma=False
    )
```

time: 260 us -> 128 us (0.49)
  the two profiles are of different devices: /device:TPU:10 before, /device:TPU:8 now
where the time goes in v1:
time: 128 us; the launch traced here: 127 us
  starting transfers between devices  44.8 us (35%)
  waiting for transfers between devices  41.8 us (33%)
  between operations  14.3 us (11%)
  Pallas kernels  12.8 us (10%)
  local copies, waits for them, and re-layouts  11.7 us (9%)
  other arithmetic  2.09 us (2%)
    ppermute x8, starting transfers between devices, moved(): lax.ppermute(value, AXES, [(i, (i + steps) % blocks) for i in range(block...  44.8 us
    all_gather x1, waiting for transfers between devices, shards(): lax.all_gather(mine.reshape(4 * panel, -1), ('core', 'mp'), axis=0, tiled...  36.5 us
    pallas_call x3, Pallas kernels, run(): pl.pallas_call(kernel, out_shape=outs, in_specs=[pl.BlockSpec(memory_spac...  12.8 us
    unnamed x20, local copies, waits for them, and re-layouts  6.85 us
    ppermute x8, waiting for transfers between devices, moved(): lax.ppermute(value, AXES, [(i, (i + steps) % blocks) for i in range(block...  5.31 us
  transfers between devices with their start and end apart: 9, of which 2 were waited for; matrix products, arithmetic and copies ran while one was open for 4% of the time, Pallas kernels for 3%

profile of v1, /device:TPU:8, one launch (start us, length us, event | category | flops | bytes accessed | tf_op | source)
XLA Modules:
  0.0 127.4 jit_solution(2922612995686548933)
XLA Ops:
  7.2 2.1 %fusion.2 = bf16[4,64,1024]{2,1,0:T(8,128)(2,1)} fusion(s32[]{:T(128)S(6)} %select_n.13, bf16[1,128,1024]{2,1,0:T(8,128)(2,1)} %bitcast.23, bf16[1,128,1024]{2,1,0:T(8,128)(2,1)} %bitcast.24, bf16[1,128,1024]{2,1,0:T(8,128)(2,1)} %bitcast.25, bf16[1,128,1024]{2,1,0:T(8,128)(2,1)} %bitcast.26), kind=kLoop, calls=%fused_computation.7 | loop fusion | flops 2097152 | bytes 1572868 | tf_op jit(solution)/shard_map/stack | solution.py:164
  9.3 0.8 reshape.65
  10.1 1.7 %gather_fusion = bf16[64,1024]{1,0:T(8,128)(2,1)S(1)} fusion(bf16[64,1024]{1,0:T(8,128)(2,1)} %nodes.3, s32[1024]{0:T(1024)S(1)} %pad_clamp_fusion), kind=kCustom, calls=%fused_computation | custom fusion | bytes 262400 | tf_op jit(solution)/shard_map/gather | solution.py:168
  11.9 3.5 %collective-permute-start = (bf16[16,1024]{1,0:T(8,128)(2,1)S(1)}, bf16[16,1024]{1,0:T(8,128)(2,1)S(1)}, u32[]{:S(2)}, u32[]{:S(2)}) collective-permute-start(bf16[16,1024]{1,0:T(8,128)(2,1)S(1)} %get-tuple-element.24), channel_id=1, source_target_pairs={{0,1},{1,2},{2,3},{3,4},{4,5},{5,6},{6,7},{7,8},{8,9},{9,10},{10,1... | collective-permute-start | bytes 98312 | tf_op jit(solution)/shard_map/ppermute | solution.py:162
  15.3 5.7 %collective-permute-start.1 = (bf16[16,1024]{1,0:T(8,128)(2,1)S(1)}, bf16[16,1024]{1,0:T(8,128)(2,1)S(1)}, u32[]{:S(2)}, u32[]{:S(2)}) collective-permute-start(bf16[16,1024]{1,0:T(8,128)(2,1)S(1)} %get-tuple-element.26), channel_id=1, source_target_pairs={{0,2},{1,3},{2,4},{3,5},{4,6},{5,7},{6,8},{7,9},{8,10},{9,11},{10,... | collective-permute-start | bytes 98312 | tf_op jit(solution)/shard_map/ppermute | solution.py:162
  21.1 6.0 %collective-permute-start.2 = (bf16[16,1024]{1,0:T(8,128)(2,1)S(1)}, bf16[16,1024]{1,0:T(8,128)(2,1)S(1)}, u32[]{:S(2)}, u32[]{:S(2)}) collective-permute-start(bf16[16,1024]{1,0:T(8,128)(2,1)S(1)} %get-tuple-element.25), channel_id=1, source_target_pairs={{0,767},{1,0},{2,1},{3,2},{4,3},{5,4},{6,5},{7,6},{8,7},{9,8},{10,... | collective-permute-start | bytes 98312 | tf_op jit(solution)/shard_map/ppermute | solution.py:162
  27.1 11.0 %collective-permute-start.3 = (bf16[16,1024]{1,0:T(8,128)(2,1)S(1)}, bf16[16,1024]{1,0:T(8,128)(2,1)S(1)}, u32[]{:S(2)}, u32[]{:S(2)}) collective-permute-start(bf16[16,1024]{1,0:T(8,128)(2,1)S(1)} %get-tuple-element.27), channel_id=1, source_target_pairs={{0,766},{1,767},{2,0},{3,1},{4,2},{5,3},{6,4},{7,5},{8,6},{9,7},{1... | collective-permute-start | bytes 98312 | tf_op jit(solution)/shard_map/ppermute | solution.py:162
  38.1 0.8 reshape.71.rows_row
  38.9 0.8 copy.17.recv_col
  39.7 0.8 copy.16.send_col
  40.5 36.5 %all-gather.2.cloned.1.call-done = bf16[4096,1024]{1,0:T(8,128)(2,1)} async-done(((bf16[256,1024]{1,0:T(8,128)(2,1)}), bf16[4096,1024]{1,0:T(8,128)(2,1)}) %all-gather.2.cloned.1.call-update) | async-done | bytes 8388624 | tf_op jit(solution)/shard_map/all_gather | solution.py:166
  77.0 0.9 copy-done
  77.9 1.0 copy-done.1
  78.9 0.9 copy-done.3
  79.8 1.0 copy-done.5
  82.8 6.5 %shard_map.147 = (bf16[192,1024]{1,0:T(8,128)(2,1)}, bf16[192,1024]{1,0:T(8,128)(2,1)S(1)}, f32[64,1024]{1,0:T(8,128)S(1)}, bf16[64,1024]{1,0:T(8,128)(2,1)S(1)}, bf16[64,1024]{1,0:T(8,128)(2,1)S(1)}) custom-call(bf16[2,8,4,64,1024]{4,3,2,1,0:T(8,128)(2,1)} %bitcast.19, bf16[64,1024]{1,0:T(8,128)(2,1)S(1)} %copy-done, ...), custom_call_target="tpu_custom_call" | custom-call | flops 1610612736 | bytes 8388608 | tf_op jit(solution)/shard_map/pallas_call | solution.py:126
  89.4 3.5 %collective-permute-start.4 = (bf16[16,1024]{1,0:T(8,128)(2,1)S(1)}, bf16[16,1024]{1,0:T(8,128)(2,1)S(1)}, u32[]{:S(2)}, u32[]{:S(2)}) collective-permute-start(bf16[16,1024]{1,0:T(8,128)(2,1)S(1)} %get-tuple-element.23), channel_id=1, source_target_pairs={{0,767},{1,0},{2,1},{3,2},{4,3},{5,4},{6,5},{7,6},{8,7},{9,8},{10,... | collective-permute-start | bytes 98312 | tf_op jit(solution)/shard_map/ppermute | solution.py:162
  92.9 10.2 %collective-permute-start.5 = (bf16[16,1024]{1,0:T(8,128)(2,1)S(1)}, bf16[16,1024]{1,0:T(8,128)(2,1)S(1)}, u32[]{:S(2)}, u32[]{:S(2)}) collective-permute-start(bf16[16,1024]{1,0:T(8,128)(2,1)S(1)} %get-tuple-element.22), channel_id=1, source_target_pairs={{0,766},{1,767},{2,0},{3,1},{4,2},{5,3},{6,4},{7,5},{8,6},{9,7},{1... | collective-permute-start | bytes 98312 | tf_op jit(solution)/shard_map/ppermute | solution.py:162
  103.1 2.9 %collective-permute-start.6 = (bf16[16,1024]{1,0:T(8,128)(2,1)S(1)}, bf16[16,1024]{1,0:T(8,128)(2,1)S(1)}, u32[]{:S(2)}, u32[]{:S(2)}) collective-permute-start(bf16[16,1024]{1,0:T(8,128)(2,1)S(1)} %get-tuple-element.21), channel_id=1, source_target_pairs={{0,1},{1,2},{2,3},{3,4},{4,5},{5,6},{6,7},{7,8},{8,9},{9,10},{10,1... | collective-permute-start | bytes 98312 | tf_op jit(solution)/shard_map/ppermute | solution.py:162
  106.0 1.9 %collective-permute-start.7 = (bf16[16,1024]{1,0:T(8,128)(2,1)S(1)}, bf16[16,1024]{1,0:T(8,128)(2,1)S(1)}, u32[]{:S(2)}, u32[]{:S(2)}) collective-permute-start(bf16[16,1024]{1,0:T(8,128)(2,1)S(1)} %get-tuple-element.20), channel_id=1, source_target_pairs={{0,2},{1,3},{2,4},{3,5},{4,6},{5,7},{6,8},{7,9},{8,10},{9,11},{10,... | collective-permute-start | bytes 98312 | tf_op jit(solution)/shard_map/ppermute | solution.py:162
  108.0 1.0 copy-done.6
  109.0 3.3 %shard_map.148 = (bf16[64,1024]{1,0:T(8,128)(2,1)}, bf16[192,1024]{1,0:T(8,128)(2,1)}, f32[64,1024]{1,0:T(8,128)S(1)}) custom-call(bf16[2,8,4,64,1024]{4,3,2,1,0:T(8,128)(2,1)} %bitcast.20, bf16[64,1024]{1,0:T(8,128)(2,1)S(1)} %copy-done, bf16[192,1024]{1,0:T(8,128)(2,1)S(1)} %copy-done.6, bf16[192,1024]{1,0:T(8,128)(2,1)S(1)} %get-tuple-element.13.grad_pre, ...), custom_call_target="tpu_custom_call" | custom-call | flops 536870912 | bytes 8388608 | tf_op jit(solution)/shard_map/pallas_call | solution.py:126
  112.3 5.3 %collective-permute-done.7.back_3 = bf16[16,1024]{1,0:T(8,128)(2,1)S(1)} collective-permute-done((bf16[16,1024]{1,0:T(8,128)(2,1)S(1)}, bf16[16,1024]{1,0:T(8,128)(2,1)S(1)}, u32[]{:S(2)}, u32[]{:S(2)}) %collective-permute-start.7) | collective-permute-done | bytes 32800 | tf_op jit(solution)/shard_map/ppermute | solution.py:162
  117.6 3.0 %shard_map.149 = bf16[64,1024]{1,0:T(8,128)(2,1)} custom-call(bf16[2,8,4,64,1024]{4,3,2,1,0:T(8,128)(2,1)} %bitcast.21, f32[64,1024]{1,0:T(8,128)S(1)} %get-tuple-element.16.own, f32[64,1024]{1,0:T(8,128)S(1)} %get-tuple-element.17.part, bf16[16,1024]{1,0:T(8,128)(2,1)S(1)} %collective-permute-done.4.back_0, ...), custom_call_target="tpu_custom_call" | custom-call | flops 134217728 | bytes 8388608 | tf_op jit(solution)/shard_map/pallas_call | solution.py:126
  (29 shorter events, 2.2 us)
Async XLA Ops:
  7.2 100.8 %copy-start.4 = (bf16[64,1024]{1,0:T(8,128)(2,1)S(1)}, bf16[64,1024]{1,0:T(8,128)(2,1)}, u32[]{:S(2)}) copy-start(bf16[64,1024]{1,0:T(8,128)(2,1)} %node_cot.3) | copy-start | bytes 393220
  7.2 100.8 %copy-start.2 = (bf16[192,1024]{1,0:T(8,128)(2,1)S(1)}, bf16[192,1024]{1,0:T(8,128)(2,1)}, u32[]{:S(2)}) copy-start(bf16[192,1024]{1,0:T(8,128)(2,1)} %edge_cot.3) | copy-start | bytes 1179652
  7.2 69.8 %all-gather.2.cloned.1.call-start = ((), (), s32[]{:S(2)}) async-start(), calls=%async_computation | async-start | bytes 8912896 | tf_op jit(solution)/shard_map/all_gather | solution.py:166
  11.9 28.6 %collective-permute-start = (bf16[16,1024]{1,0:T(8,128)(2,1)S(1)}, bf16[16,1024]{1,0:T(8,128)(2,1)S(1)}, u32[]{:S(2)}, u32[]{:S(2)}) collective-permute-start(bf16[16,1024]{1,0:T(8,128)(2,1)S(1)} %get-tuple-element.24), channel_id=1, source_target_pairs={{0,1},{1,2},{2,3},{3,4},{4,5},{5,6},{6,7},{7,8},{8,9},{9,10},{10,1... | collective-permute-start | bytes 98312 | tf_op jit(solution)/shard_map/ppermute | solution.py:162
  15.3 25.1 %collective-permute-start.1 = (bf16[16,1024]{1,0:T(8,128)(2,1)S(1)}, bf16[16,1024]{1,0:T(8,128)(2,1)S(1)}, u32[]{:S(2)}, u32[]{:S(2)}) collective-permute-start(bf16[16,1024]{1,0:T(8,128)(2,1)S(1)} %get-tuple-element.26), channel_id=1, source_target_pairs={{0,2},{1,3},{2,4},{3,5},{4,6},{5,7},{6,8},{7,9},{8,10},{9,11},{10,... | collective-permute-start | bytes 98312 | tf_op jit(solution)/shard_map/ppermute | solution.py:162
  21.1 19.4 %collective-permute-start.2 = (bf16[16,1024]{1,0:T(8,128)(2,1)S(1)}, bf16[16,1024]{1,0:T(8,128)(2,1)S(1)}, u32[]{:S(2)}, u32[]{:S(2)}) collective-permute-start(bf16[16,1024]{1,0:T(8,128)(2,1)S(1)} %get-tuple-element.25), channel_id=1, source_target_pairs={{0,767},{1,0},{2,1},{3,2},{4,3},{5,4},{6,5},{7,6},{8,7},{9,8},{10,... | collective-permute-start | bytes 98312 | tf_op jit(solution)/shard_map/ppermute | solution.py:162
  27.1 13.4 %collective-permute-start.3 = (bf16[16,1024]{1,0:T(8,128)(2,1)S(1)}, bf16[16,1024]{1,0:T(8,128)(2,1)S(1)}, u32[]{:S(2)}, u32[]{:S(2)}) collective-permute-start(bf16[16,1024]{1,0:T(8,128)(2,1)S(1)} %get-tuple-element.27), channel_id=1, source_target_pairs={{0,766},{1,767},{2,0},{3,1},{4,2},{5,3},{6,4},{7,5},{8,6},{9,7},{1... | collective-permute-start | bytes 98312 | tf_op jit(solution)/shard_map/ppermute | solution.py:162
  77.0 0.9 copy-start
  77.9 1.0 copy-start.1
  78.9 0.9 copy-start.3
  79.8 1.0 copy-start.5
  80.8 0.7 copy-start.7
  81.5 0.7 copy-start.8
  82.2 0.7 copy-start.9
  89.4 22.9 %collective-permute-start.4 = (bf16[16,1024]{1,0:T(8,128)(2,1)S(1)}, bf16[16,1024]{1,0:T(8,128)(2,1)S(1)}, u32[]{:S(2)}, u32[]{:S(2)}) collective-permute-start(bf16[16,1024]{1,0:T(8,128)(2,1)S(1)} %get-tuple-element.23), channel_id=1, source_target_pairs={{0,767},{1,0},{2,1},{3,2},{4,3},{5,4},{6,5},{7,6},{8,7},{9,8},{10,... | collective-permute-start | bytes 98312 | tf_op jit(solution)/shard_map/ppermute | solution.py:162
  92.9 19.4 %collective-permute-start.5 = (bf16[16,1024]{1,0:T(8,128)(2,1)S(1)}, bf16[16,1024]{1,0:T(8,128)(2,1)S(1)}, u32[]{:S(2)}, u32[]{:S(2)}) collective-permute-start(bf16[16,1024]{1,0:T(8,128)(2,1)S(1)} %get-tuple-element.22), channel_id=1, source_target_pairs={{0,766},{1,767},{2,0},{3,1},{4,2},{5,3},{6,4},{7,5},{8,6},{9,7},{1... | collective-permute-start | bytes 98312 | tf_op jit(solution)/shard_map/ppermute | solution.py:162
  103.1 9.2 %collective-permute-start.6 = (bf16[16,1024]{1,0:T(8,128)(2,1)S(1)}, bf16[16,1024]{1,0:T(8,128)(2,1)S(1)}, u32[]{:S(2)}, u32[]{:S(2)}) collective-permute-start(bf16[16,1024]{1,0:T(8,128)(2,1)S(1)} %get-tuple-element.21), channel_id=1, source_target_pairs={{0,1},{1,2},{2,3},{3,4},{4,5},{5,6},{6,7},{7,8},{8,9},{9,10},{10,1... | collective-permute-start | bytes 98312 | tf_op jit(solution)/shard_map/ppermute | solution.py:162
  106.0 11.6 %collective-permute-start.7 = (bf16[16,1024]{1,0:T(8,128)(2,1)S(1)}, bf16[16,1024]{1,0:T(8,128)(2,1)S(1)}, u32[]{:S(2)}, u32[]{:S(2)}) collective-permute-start(bf16[16,1024]{1,0:T(8,128)(2,1)S(1)} %get-tuple-element.20), channel_id=1, source_target_pairs={{0,2},{1,3},{2,4},{3,5},{4,6},{5,7},{6,8},{7,9},{8,10},{9,11},{10,... | collective-permute-start | bytes 98312 | tf_op jit(solution)/shard_map/ppermute | solution.py:162
  108.0 1.0 copy-start.6
Sparse Core Ops, SparseCore 0:
  10.4 66.5 all-gather.1

commit v2 on v1

v2 whole, which is shorter than its diff:
```python
import jax
import jax.numpy as jnp
from jax import lax
from jax.experimental import pallas as pl
from jax.experimental.pallas import tpu as pltpu
from jax.sharding import Mesh, PartitionSpec as P

eps = 1e-05
BF = jnp.bfloat16
F32 = jnp.float32
AXES = ("rest", "core", "mp")
EDGE, SEND, RECEIVE, OUTPUT = 0, 1, 2, 3
HBM = pl.BlockSpec(memory_space=pltpu.HBM)
VMEM_BYTES = 56 * 1024 * 1024


def dot(left, right):
    return jnp.dot(left, right, preferred_element_type=F32)


def dot_rows(left, right):
    return lax.dot_general(left, right, (((1,), (1,)), ((), ())), preferred_element_type=F32)


def fetches(panels, held, sems, which):
    return [
        pltpu.make_async_copy(panels.at[core, :, which], held.at[:, core], sems.at[core])
        for core in range(2)
    ]


def begin(copies):
    for copy in copies:
        copy.start()


def finish(copies):
    for copy in copies:
        copy.wait()


def matrix(held):
    value = held[...]
    return value.reshape(-1, value.shape[-1])


def one_hot_t(ids_row, count):
    columns = ids_row.shape[1]
    return (lax.broadcasted_iota(jnp.int32, (count, columns), 0) == ids_row).astype(F32).astype(BF)


def picked(hot, table):
    return lax.dot_general(hot, table, (((0,), (0,)), ((), ())), preferred_element_type=F32)


def loads(pairs, sems):
    return [pltpu.make_async_copy(s, d, sems.at[i]) for i, (s, d) in enumerate(pairs)]


def pick_kernel(nodes, send_rows, *outs):
    for j, out in enumerate(outs):
        out[...] = picked(one_hot_t(send_rows[j : j + 1], nodes.shape[0]), nodes[...]).astype(BF)


def edge_kernel(
    panels, nodes_in, halo_0, halo_1, halo_2, halo_3, edges_in, gain_in, send_row_in, recv_row_in, node_cot_in, edge_cot_in,
    new_nodes, new_edges, grad_pre, own, out_0, out_1, out_2, out_3, grad_recv,
    w_send, w_recv, w_edge, w_out, table_rows, edges, gain, send_row, recv_row, node_cot, edge_cot,
    sems, small_sems,
):
    node_count, halo = nodes_in.shape[0], halo_0.shape[0]
    table = table_rows.shape[0]
    first = [(nodes_in, table_rows.at[pl.ds(0, node_count)])]
    for j, rows in enumerate((halo_0, halo_1, halo_2, halo_3)):
        first.append((rows, table_rows.at[pl.ds(node_count + j * halo, halo)]))
    rest = [(recv_row_in, recv_row), (send_row_in, send_row), (node_cot_in, node_cot), (edge_cot_in, edge_cot)]
    rest += [(gain_in, gain), (edges_in, edges)]
    small = loads(first + rest, small_sems)
    order = ((w_send, SEND), (w_recv, RECEIVE), (w_edge, EDGE), (w_out, OUTPUT))
    copies = [fetches(panels, held, sems.at[i], which) for i, (held, which) in enumerate(order)]
    begin(small[: len(first)])
    begin(copies[0])
    begin(small[len(first) :])
    for pair in copies[1:]:
        begin(pair)
    finish(small[: len(first)])
    finish(copies[0])
    lookup = dot(table_rows[...], matrix(w_send)).astype(BF)
    finish(small[len(first) :])
    to_recv = one_hot_t(recv_row[...], node_count)
    to_send = one_hot_t(send_row[...], table)
    grad_total = edge_cot[...].astype(F32) + picked(to_recv, node_cot[...])
    finish(copies[1])
    received = dot(table_rows[:node_count], matrix(w_recv)).astype(BF)
    finish(copies[2])
    preact = dot(edges[...], matrix(w_edge))
    preact = preact + picked(to_send, lookup)
    preact = preact + picked(to_recv, received)
    gate = 1.0 / (1.0 + jnp.exp(-preact))
    hidden = (preact * gate).astype(BF)
    slope = gate * (1.0 + preact * (1.0 - gate))
    finish(copies[3])
    projected = dot(hidden, matrix(w_out))
    centred = projected - jnp.mean(projected, axis=-1, keepdims=True)
    scale = lax.rsqrt(jnp.mean(centred * centred, axis=-1, keepdims=True) + eps)
    normal = centred * scale
    edges_out = (edges[...].astype(F32) + normal * gain[...]).astype(BF)
    new_edges[...] = edges_out
    new_nodes[...] = (table_rows[:node_count].astype(F32) + dot(to_recv, edges_out)).astype(BF)
    pulled = grad_total * gain[...]
    mean_pulled = jnp.mean(pulled, axis=-1, keepdims=True)
    mean_along = jnp.mean(pulled * normal, axis=-1, keepdims=True)
    grad_projected = (scale * (pulled - mean_pulled - normal * mean_along)).astype(BF)
    grad_preact = (dot_rows(grad_projected, matrix(w_out)) * slope).astype(BF)
    grad_pre[...] = grad_preact
    grad_lookup = dot(to_send, grad_preact)
    own[...] = grad_lookup[:node_count]
    for j, out in enumerate((out_0, out_1, out_2, out_3)):
        out[...] = grad_lookup[node_count + j * halo : node_count + (j + 1) * halo].astype(BF)
    grad_recv[...] = dot(to_recv, grad_preact).astype(BF)


def local_kernel(
    panels, grad_pre_in, grad_recv_in, recv_row_in, node_cot_in, edge_cot_in, grad_edges, part,
    w_edge, w_recv, grad_pre, grad_recv, recv_row, node_cot, edge_cot, sems, small_sems,
):
    small = loads(
        ((grad_pre_in, grad_pre), (recv_row_in, recv_row), (node_cot_in, node_cot), (edge_cot_in, edge_cot),
         (grad_recv_in, grad_recv)),
        small_sems,
    )
    copies = [fetches(panels, w_edge, sems.at[0], EDGE), fetches(panels, w_recv, sems.at[1], RECEIVE)]
    begin(copies[0])
    begin(small)
    begin(copies[1])
    finish(small)
    to_recv = one_hot_t(recv_row[...], node_cot.shape[0])
    grad_total = edge_cot[...].astype(F32) + picked(to_recv, node_cot[...])
    finish(copies[0])
    grad_edges[...] = (grad_total + dot_rows(grad_pre[...], matrix(w_edge))).astype(BF)
    finish(copies[1])
    part[...] = node_cot[...].astype(F32) + dot_rows(grad_recv[...], matrix(w_recv))


def node_kernel(
    panels, own_in, part_in, rows_in, back_0, back_1, back_2, back_3, grad_nodes,
    w_send, own, part, rows, b_0, b_1, b_2, b_3, sems, small_sems,
):
    ins = (back_0, back_1, back_2, back_3, rows_in, own_in, part_in)
    small = loads(list(zip(ins, (b_0, b_1, b_2, b_3, rows, own, part))), small_sems)
    copies = fetches(panels, w_send, sems.at[0], SEND)
    begin(copies)
    begin(small)
    finish(small)
    grad_send = own[...]
    for j, back in enumerate((b_0, b_1, b_2, b_3)):
        grad_send = grad_send + dot(one_hot_t(rows[j : j + 1], own.shape[0]), back[...])
    finish(copies)
    grad_nodes[...] = (part[...] + dot_rows(grad_send.astype(BF), matrix(w_send))).astype(BF)


def run(kernel, outs, weights, flops, panels, values, kept):
    cores, groups, _, panel, width = panels.shape
    return pl.pallas_call(
        kernel,
        out_shape=outs,
        in_specs=[HBM] * (1 + len(values)),
        out_specs=jax.tree.map(lambda _: pl.BlockSpec(memory_space=pltpu.VMEM), outs),
        scratch_shapes=[pltpu.VMEM((groups, cores, panel, width), BF)] * weights
        + [pltpu.VMEM(k.shape, k.dtype) for k in kept]
        + [pltpu.SemaphoreType.DMA((weights, cores)), pltpu.SemaphoreType.DMA((len(values),))],
        compiler_params=pltpu.CompilerParams(vmem_limit_bytes=VMEM_BYTES),
        cost_estimate=pl.CostEstimate(flops=flops, bytes_accessed=4 * 2**20, transcendentals=0),
    )(panels, *values)


def shards(
    node_states,
    edge_states,
    edge_weight,
    send_weight,
    receive_weight,
    output_weight,
    norm_gain,
    senders,
    receivers,
    send_rows,
    node_cotangent,
    edge_cotangent,
):
    nodes, width = node_states.shape
    edges = edge_states.shape[0]
    spread, halo = send_rows.shape[1] // 2, send_rows.shape[2]
    shifts = [step + 1 for step in range(spread)] + [-(step + 1) for step in range(spread)]
    blocks = lax.axis_size(AXES)
    groups = lax.axis_size("mp")
    panel = edge_weight.shape[0] // 2
    core = lax.axis_index("core")

    def moved(value, steps):
        return lax.ppermute(value, AXES, [(i, (i + steps) % blocks) for i in range(blocks)])

    weights = jnp.stack([edge_weight, send_weight, receive_weight, output_weight])
    mine = lax.dynamic_slice_in_dim(weights, core * panel, panel, axis=1)
    gathered = lax.all_gather(mine.reshape(4 * panel, -1), ("core", "mp"), axis=0, tiled=True)
    panels = gathered.reshape(2, groups, 4, panel, -1)
    rows_by_shift = send_rows.reshape(2 * spread, halo)

    def rows(count, kind=BF):
        return jax.ShapeDtypeStruct((count, width), kind)

    halo_rows = (rows(halo),) * (2 * spread)
    chosen = pl.pallas_call(pick_kernel, out_shape=halo_rows)(node_states, rows_by_shift)
    arrived = [moved(chosen[j], shifts[j]) for j in range(2 * spread)]
    gain = norm_gain.reshape(1, -1)
    send_row, recv_row = senders.reshape(1, -1), receivers.reshape(1, -1)
    new_nodes, new_edges, grad_pre, own, *outgoing, grad_recv = run(
        edge_kernel,
        (rows(nodes), rows(edges), rows(edges), rows(nodes, F32), *halo_rows, rows(nodes)),
        4,
        2 * 768 * width * width,
        panels,
        [node_states, *arrived, edge_states, gain, send_row, recv_row, node_cotangent, edge_cotangent],
        [rows(nodes + 2 * spread * halo), edge_states, gain, send_row, recv_row, node_cotangent, edge_cotangent],
    )
    back = [moved(outgoing[j], -shifts[j]) for j in range(2 * spread)]
    near = [grad_pre, grad_recv, recv_row, node_cotangent, edge_cotangent]
    grad_edges, part = run(
        local_kernel, (rows(edges), rows(nodes, F32)), 2, 2 * 256 * width * width, panels, near, near
    )
    last = [own, part, rows_by_shift, *back]
    grad_nodes = run(
        node_kernel, rows(nodes), 1, 2 * 64 * width * width, panels, last, last
    )
    return new_nodes, new_edges, grad_nodes, grad_edges


def solution(mesh):
    split = Mesh(mesh.devices.reshape(-1, 2, mesh.shape["mp"]), AXES)
    rows_spec, panel_spec = P(AXES, None), P("mp", None)
    in_specs = (
        rows_spec,
        rows_spec,
        panel_spec,
        panel_spec,
        panel_spec,
        panel_spec,
        P(),
        P(AXES),
        P(AXES),
        P(AXES, None, None),
        rows_spec,
        rows_spec,
    )
    return jax.shard_map(
        shards, mesh=split, in_specs=in_specs, out_specs=(rows_spec,) * 4, check_vma=False
    )
```

time: 128 us -> 125 us (0.977)
  local copies, waits for them, and re-layouts: 11.7 us -> 0.62 us
  Pallas kernels: 12.8 us -> 18.3 us
  waiting for transfers between devices: 41.8 us -> 44.7 us
    unnamed x20 -> x16, local copies, waits for them, and re-layouts: 6.85 us -> 0.62 us
    pallas_call x3 -> x4, Pallas kernels: 12.8 us -> 18.3 us  [the longest x3 16.6 us: run(): pl.pallas_call(kernel, out_shape=outs, in_specs=[HBM] * (1 + len(values))...]
    reshape x4 -> x0, local copies, waits for them, and re-layouts: 3.12 us -> none  [the longest x1 0.79 us: shards(): send_col, send_row = (senders.reshape(-1, 1), senders.reshape(1, -1))]
    gather x1 -> x0, local copies, waits for them, and re-layouts: 1.72 us -> none  [shards(): chosen = node_states.at[send_rows.reshape(-1)].get(mode='promise_in_bounds')]
    ppermute x8, waiting for transfers between devices: 5.31 us -> 6.87 us  [moved(): lax.ppermute(value, AXES, [(i, (i + steps) % blocks) for i in range(block...]
    all_gather x1, waiting for transfers between devices: 36.5 us -> 37.9 us  [shards(): lax.all_gather(mine.reshape(4 * panel, -1), ('core', 'mp'), axis=0, tiled...]
  transfers between devices with their start and end apart: 9 -> 9, of which waited for: 2 -> 3; matrix products, arithmetic and copies ran while one was open for 4% -> 0% of each run, Pallas kernels for 3% -> 5%
where the time goes in v2:
time: 125 us
  starting transfers between devices  44.8 us (36%)
  waiting for transfers between devices  44.7 us (36%)
  Pallas kernels  18.3 us (15%)
  between operations  14.2 us (11%)
  other arithmetic  1.98 us (2%)
    ppermute x8, starting transfers between devices, moved(): lax.ppermute(value, AXES, [(i, (i + steps) % blocks) for i in range(block...  44.7 us
    all_gather x1, waiting for transfers between devices, shards(): lax.all_gather(mine.reshape(4 * panel, -1), ('core', 'mp'), axis=0, tiled...  37.9 us
    pallas_call x3, Pallas kernels, run(): pl.pallas_call(kernel, out_shape=outs, in_specs=[HBM] * (1 + len(values))...  16.6 us
    ppermute x8, waiting for transfers between devices, moved(): lax.ppermute(value, AXES, [(i, (i + steps) % blocks) for i in range(block...  6.87 us
  transfers between devices with their start and end apart: 9, of which 3 were waited for; matrix products, arithmetic and copies ran while one was open for 0% of the time, Pallas kernels for 5%

profile of v2, /device:TPU:8, one launch (start us, length us, event | category | flops | bytes accessed | tf_op | source)
XLA Modules:
  0.0 124.7 jit_solution(12025155916512256940)
XLA Ops:
  7.2 0.0 all-gather.2.cloned.1.call-start
  7.2 2.0 %fusion.2 = bf16[4,64,1024]{2,1,0:T(8,128)(2,1)} fusion(s32[]{:T(128)S(6)} %select_n.3, bf16[1,128,1024]{2,1,0:T(8,128)(2,1)} %bitcast.14, bf16[1,128,1024]{2,1,0:T(8,128)(2,1)} %bitcast.15, bf16[1,128,1024]{2,1,0:T(8,128)(2,1)} %bitcast.16, bf16[1,128,1024]{2,1,0:T(8,128)(2,1)} %bitcast.17), kind=kLoop, calls=%fused_computation.6 | loop fusion | flops 2097152 | bytes 1572868 | tf_op jit(solution)/shard_map/stack | solution.py:203
  9.2 0.0 all-gather.2.cloned.1.call-update
  9.2 1.8 %shard_map.147 = (bf16[16,1024]{1,0:T(8,128)(2,1)}, bf16[16,1024]{1,0:T(8,128)(2,1)}, bf16[16,1024]{1,0:T(8,128)(2,1)}, bf16[16,1024]{1,0:T(8,128)(2,1)}) custom-call(bf16[64,1024]{1,0:T(8,128)(2,1)} %nodes_in.1, s32[4,16]{1,0:T(4,128)} %bitcast.18), custom_call_target="tpu_custom_call" | custom-call | tf_op jit(solution)/shard_map/pallas_call | solution.py:213
  11.0 3.5 %collective-permute-start = (bf16[16,1024]{1,0:T(8,128)(2,1)}, bf16[16,1024]{1,0:T(8,128)(2,1)S(1)}, u32[]{:S(2)}, u32[]{:S(2)}) collective-permute-start(bf16[16,1024]{1,0:T(8,128)(2,1)} %get-tuple-element.19), channel_id=1, source_target_pairs={{0,1},{1,2},{2,3},{3,4},{4,5},{5,6},{6,7},{7,8},{8,9},{9,10},{10,1... | collective-permute-start | bytes 98312 | tf_op jit(solution)/shard_map/ppermute | solution.py:201
  14.5 5.7 %collective-permute-start.1 = (bf16[16,1024]{1,0:T(8,128)(2,1)}, bf16[16,1024]{1,0:T(8,128)(2,1)S(1)}, u32[]{:S(2)}, u32[]{:S(2)}) collective-permute-start(bf16[16,1024]{1,0:T(8,128)(2,1)} %get-tuple-element.20), channel_id=1, source_target_pairs={{0,2},{1,3},{2,4},{3,5},{4,6},{5,7},{6,8},{7,9},{8,10},{9,11},{10,... | collective-permute-start | bytes 98312 | tf_op jit(solution)/shard_map/ppermute | solution.py:201
  20.2 6.0 %collective-permute-start.2 = (bf16[16,1024]{1,0:T(8,128)(2,1)}, bf16[16,1024]{1,0:T(8,128)(2,1)S(1)}, u32[]{:S(2)}, u32[]{:S(2)}) collective-permute-start(bf16[16,1024]{1,0:T(8,128)(2,1)} %get-tuple-element.21), channel_id=1, source_target_pairs={{0,767},{1,0},{2,1},{3,2},{4,3},{5,4},{6,5},{7,6},{8,7},{9,8},{10,... | collective-permute-start | bytes 98312 | tf_op jit(solution)/shard_map/ppermute | solution.py:201
  26.2 11.0 %collective-permute-start.3 = (bf16[16,1024]{1,0:T(8,128)(2,1)}, bf16[16,1024]{1,0:T(8,128)(2,1)S(1)}, u32[]{:S(2)}, u32[]{:S(2)}) collective-permute-start(bf16[16,1024]{1,0:T(8,128)(2,1)} %get-tuple-element.22), channel_id=1, source_target_pairs={{0,766},{1,767},{2,0},{3,1},{4,2},{5,3},{6,4},{7,5},{8,6},{9,7},{1... | collective-permute-start | bytes 98312 | tf_op jit(solution)/shard_map/ppermute | solution.py:201
  37.2 0.0 collective-permute-done.halo_0
  37.2 0.0 collective-permute-done.1.halo_1
  37.3 0.0 copy-start.2
  37.3 1.8 %collective-permute-done.3.halo_3 = bf16[16,1024]{1,0:T(8,128)(2,1)S(1)} collective-permute-done((bf16[16,1024]{1,0:T(8,128)(2,1)}, bf16[16,1024]{1,0:T(8,128)(2,1)S(1)}, u32[]{:S(2)}, u32[]{:S(2)}) %collective-permute-start.3) | collective-permute-done | bytes 32800 | tf_op jit(solution)/shard_map/ppermute | solution.py:201
  39.1 37.9 %all-gather.2.cloned.1.call-done = bf16[4096,1024]{1,0:T(8,128)(2,1)} async-done(((bf16[256,1024]{1,0:T(8,128)(2,1)}), bf16[4096,1024]{1,0:T(8,128)(2,1)}) %all-gather.2.cloned.1.call-update) | async-done | bytes 8388624 | tf_op jit(solution)/shard_map/all_gather | solution.py:205
  77.0 8.3 %shard_map.148 = (bf16[64,1024]{1,0:T(8,128)(2,1)}, bf16[192,1024]{1,0:T(8,128)(2,1)}, bf16[192,1024]{1,0:T(8,128)(2,1)}, f32[64,1024]{1,0:T(8,128)}, bf16[16,10...) custom-call(bf16[2,8,4,64,1024]{4,3,2,1,0:T(8,128)(2,1)} %bitcast.10, ...), custom_call_target="tpu_custom_call" | custom-call | flops 1610612736 | bytes 4194304 | tf_op jit(solution)/shard_map/pallas_call | solution.py:164
  85.3 3.5 %collective-permute-start.4 = (bf16[16,1024]{1,0:T(8,128)(2,1)}, bf16[16,1024]{1,0:T(8,128)(2,1)S(1)}, u32[]{:S(2)}, u32[]{:S(2)}) collective-permute-start(bf16[16,1024]{1,0:T(8,128)(2,1)} %get-tuple-element.29), channel_id=1, source_target_pairs={{0,767},{1,0},{2,1},{3,2},{4,3},{5,4},{6,5},{7,6},{8,7},{9,8},{10,... | collective-permute-start | bytes 98312 | tf_op jit(solution)/shard_map/ppermute | solution.py:201
  88.8 10.1 %collective-permute-start.5 = (bf16[16,1024]{1,0:T(8,128)(2,1)}, bf16[16,1024]{1,0:T(8,128)(2,1)S(1)}, u32[]{:S(2)}, u32[]{:S(2)}) collective-permute-start(bf16[16,1024]{1,0:T(8,128)(2,1)} %get-tuple-element.30), channel_id=1, source_target_pairs={{0,766},{1,767},{2,0},{3,1},{4,2},{5,3},{6,4},{7,5},{8,6},{9,7},{1... | collective-permute-start | bytes 98312 | tf_op jit(solution)/shard_map/ppermute | solution.py:201
  98.9 3.0 %collective-permute-start.6 = (bf16[16,1024]{1,0:T(8,128)(2,1)}, bf16[16,1024]{1,0:T(8,128)(2,1)S(1)}, u32[]{:S(2)}, u32[]{:S(2)}) collective-permute-start(bf16[16,1024]{1,0:T(8,128)(2,1)} %get-tuple-element.31), channel_id=1, source_target_pairs={{0,1},{1,2},{2,3},{3,4},{4,5},{5,6},{6,7},{7,8},{8,9},{9,10},{10,1... | collective-permute-start | bytes 98312 | tf_op jit(solution)/shard_map/ppermute | solution.py:201
  101.9 1.9 %collective-permute-start.7 = (bf16[16,1024]{1,0:T(8,128)(2,1)}, bf16[16,1024]{1,0:T(8,128)(2,1)S(1)}, u32[]{:S(2)}, u32[]{:S(2)}) collective-permute-start(bf16[16,1024]{1,0:T(8,128)(2,1)} %get-tuple-element.32), channel_id=1, source_target_pairs={{0,2},{1,3},{2,4},{3,5},{4,6},{5,7},{6,8},{7,9},{8,10},{9,11},{10,... | collective-permute-start | bytes 98312 | tf_op jit(solution)/shard_map/ppermute | solution.py:201
  103.9 4.8 %shard_map.149 = (bf16[192,1024]{1,0:T(8,128)(2,1)}, f32[64,1024]{1,0:T(8,128)}) custom-call(bf16[2,8,4,64,1024]{4,3,2,1,0:T(8,128)(2,1)} %bitcast.11, bf16[192,1024]{1,0:T(8,128)(2,1)} %get-tuple-element.26.grad_pre_in, bf16[64,1024]{1,0:T(8,128)(2,1)} %get-tuple-element.27.grad_recv_in, s32[1,192]{1,0:T(1,128)} %bitcast.22, bf16[64,1024]{1,0:T(8,128)(2,1)} %node_cot_in.3, ...), custom_call_target="tpu_custom_call" | custom-call | flops 536870912 | bytes 4194304 | tf_op jit(solution)/shard_map/pallas_call | solution.py:164
  108.6 0.0 collective-permute-done.4.back_0
  108.7 0.0 collective-permute-done.6.back_2
  108.7 5.0 %collective-permute-done.7.back_3 = bf16[16,1024]{1,0:T(8,128)(2,1)S(1)} collective-permute-done((bf16[16,1024]{1,0:T(8,128)(2,1)}, bf16[16,1024]{1,0:T(8,128)(2,1)S(1)}, u32[]{:S(2)}, u32[]{:S(2)}) %collective-permute-start.7) | collective-permute-done | bytes 32800 | tf_op jit(solution)/shard_map/ppermute | solution.py:201
  113.7 0.6 copy-done.7
  114.3 3.5 %shard_map.150 = bf16[64,1024]{1,0:T(8,128)(2,1)} custom-call(bf16[2,8,4,64,1024]{4,3,2,1,0:T(8,128)(2,1)} %bitcast.12, f32[64,1024]{1,0:T(8,128)} %get-tuple-element.25.own_in, f32[64,1024]{1,0:T(8,128)} %get-tuple-element.28.part_in, s32[4,16]{1,0:T(4,128)} %bitcast.19, bf16[16,1024]{1,0:T(8,128)(2,1)} %copy-done.3, bf16[16,1024]{1,0:T(8,128)(2,1)} %copy-done.5, ...), custom_call_target="tpu_custom_call" | custom-call | flops 134217728 | bytes 4194304 | tf_op jit(solution)/shard_map/pallas_call | solution.py:164
  (16 shorter events, 0.0 us)
Async XLA Ops:
  7.2 69.8 %all-gather.2.cloned.1.call-start = ((), (), s32[]{:S(2)}) async-start(), calls=%async_computation | async-start | bytes 8912896 | tf_op jit(solution)/shard_map/all_gather | solution.py:205
  11.0 26.2 %collective-permute-start = (bf16[16,1024]{1,0:T(8,128)(2,1)}, bf16[16,1024]{1,0:T(8,128)(2,1)S(1)}, u32[]{:S(2)}, u32[]{:S(2)}) collective-permute-start(bf16[16,1024]{1,0:T(8,128)(2,1)} %get-tuple-element.19), channel_id=1, source_target_pairs={{0,1},{1,2},{2,3},{3,4},{4,5},{5,6},{6,7},{7,8},{8,9},{9,10},{10,1... | collective-permute-start | bytes 98312 | tf_op jit(solution)/shard_map/ppermute | solution.py:201
  14.5 22.8 %collective-permute-start.1 = (bf16[16,1024]{1,0:T(8,128)(2,1)}, bf16[16,1024]{1,0:T(8,128)(2,1)S(1)}, u32[]{:S(2)}, u32[]{:S(2)}) collective-permute-start(bf16[16,1024]{1,0:T(8,128)(2,1)} %get-tuple-element.20), channel_id=1, source_target_pairs={{0,2},{1,3},{2,4},{3,5},{4,6},{5,7},{6,8},{7,9},{8,10},{9,11},{10,... | collective-permute-start | bytes 98312 | tf_op jit(solution)/shard_map/ppermute | solution.py:201
  20.2 17.1 %collective-permute-start.2 = (bf16[16,1024]{1,0:T(8,128)(2,1)}, bf16[16,1024]{1,0:T(8,128)(2,1)S(1)}, u32[]{:S(2)}, u32[]{:S(2)}) collective-permute-start(bf16[16,1024]{1,0:T(8,128)(2,1)} %get-tuple-element.21), channel_id=1, source_target_pairs={{0,767},{1,0},{2,1},{3,2},{4,3},{5,4},{6,5},{7,6},{8,7},{9,8},{10,... | collective-permute-start | bytes 98312 | tf_op jit(solution)/shard_map/ppermute | solution.py:201
  26.2 12.9 %collective-permute-start.3 = (bf16[16,1024]{1,0:T(8,128)(2,1)}, bf16[16,1024]{1,0:T(8,128)(2,1)S(1)}, u32[]{:S(2)}, u32[]{:S(2)}) collective-permute-start(bf16[16,1024]{1,0:T(8,128)(2,1)} %get-tuple-element.22), channel_id=1, source_target_pairs={{0,766},{1,767},{2,0},{3,1},{4,2},{5,3},{6,4},{7,5},{8,6},{9,7},{1... | collective-permute-start | bytes 98312 | tf_op jit(solution)/shard_map/ppermute | solution.py:201
  37.2 39.7 %copy-start = (bf16[16,1024]{1,0:T(8,128)(2,1)}, bf16[16,1024]{1,0:T(8,128)(2,1)S(1)}, u32[]{:S(2)}) copy-start(bf16[16,1024]{1,0:T(8,128)(2,1)S(1)} %collective-permute-done.halo_0) | copy-start | bytes 98308
  37.3 39.7 %copy-start.1 = (bf16[16,1024]{1,0:T(8,128)(2,1)}, bf16[16,1024]{1,0:T(8,128)(2,1)S(1)}, u32[]{:S(2)}) copy-start(bf16[16,1024]{1,0:T(8,128)(2,1)S(1)} %collective-permute-done.1.halo_1) | copy-start | bytes 98308
  37.3 39.7 %copy-start.2 = (bf16[16,1024]{1,0:T(8,128)(2,1)}, bf16[16,1024]{1,0:T(8,128)(2,1)S(1)}, u32[]{:S(2)}) copy-start(bf16[16,1024]{1,0:T(8,128)(2,1)S(1)} %collective-permute-done.2.halo_2) | copy-start | bytes 98308
  39.1 37.9 %copy-start.4 = (bf16[16,1024]{1,0:T(8,128)(2,1)}, bf16[16,1024]{1,0:T(8,128)(2,1)S(1)}, u32[]{:S(2)}) copy-start(bf16[16,1024]{1,0:T(8,128)(2,1)S(1)} %collective-permute-done.3.halo_3) | copy-start | bytes 98308
  85.3 23.3 %collective-permute-start.4 = (bf16[16,1024]{1,0:T(8,128)(2,1)}, bf16[16,1024]{1,0:T(8,128)(2,1)S(1)}, u32[]{:S(2)}, u32[]{:S(2)}) collective-permute-start(bf16[16,1024]{1,0:T(8,128)(2,1)} %get-tuple-element.29), channel_id=1, source_target_pairs={{0,767},{1,0},{2,1},{3,2},{4,3},{5,4},{6,5},{7,6},{8,7},{9,8},{10,... | collective-permute-start | bytes 98312 | tf_op jit(solution)/shard_map/ppermute | solution.py:201
  88.8 19.8 %collective-permute-start.5 = (bf16[16,1024]{1,0:T(8,128)(2,1)}, bf16[16,1024]{1,0:T(8,128)(2,1)S(1)}, u32[]{:S(2)}, u32[]{:S(2)}) collective-permute-start(bf16[16,1024]{1,0:T(8,128)(2,1)} %get-tuple-element.30), channel_id=1, source_target_pairs={{0,766},{1,767},{2,0},{3,1},{4,2},{5,3},{6,4},{7,5},{8,6},{9,7},{1... | collective-permute-start | bytes 98312 | tf_op jit(solution)/shard_map/ppermute | solution.py:201
  98.9 9.8 %collective-permute-start.6 = (bf16[16,1024]{1,0:T(8,128)(2,1)}, bf16[16,1024]{1,0:T(8,128)(2,1)S(1)}, u32[]{:S(2)}, u32[]{:S(2)}) collective-permute-start(bf16[16,1024]{1,0:T(8,128)(2,1)} %get-tuple-element.31), channel_id=1, source_target_pairs={{0,1},{1,2},{2,3},{3,4},{4,5},{5,6},{6,7},{7,8},{8,9},{9,10},{10,1... | collective-permute-start | bytes 98312 | tf_op jit(solution)/shard_map/ppermute | solution.py:201
  101.9 11.8 %collective-permute-start.7 = (bf16[16,1024]{1,0:T(8,128)(2,1)}, bf16[16,1024]{1,0:T(8,128)(2,1)S(1)}, u32[]{:S(2)}, u32[]{:S(2)}) collective-permute-start(bf16[16,1024]{1,0:T(8,128)(2,1)} %get-tuple-element.32), channel_id=1, source_target_pairs={{0,2},{1,3},{2,4},{3,5},{4,6},{5,7},{6,8},{7,9},{8,10},{9,11},{10,... | collective-permute-start | bytes 98312 | tf_op jit(solution)/shard_map/ppermute | solution.py:201
  108.6 5.1 %copy-start.3 = (bf16[16,1024]{1,0:T(8,128)(2,1)}, bf16[16,1024]{1,0:T(8,128)(2,1)S(1)}, u32[]{:S(2)}) copy-start(bf16[16,1024]{1,0:T(8,128)(2,1)S(1)} %collective-permute-done.4.back_0) | copy-start | bytes 98308
  108.7 5.1 %copy-start.5 = (bf16[16,1024]{1,0:T(8,128)(2,1)}, bf16[16,1024]{1,0:T(8,128)(2,1)S(1)}, u32[]{:S(2)}) copy-start(bf16[16,1024]{1,0:T(8,128)(2,1)S(1)} %collective-permute-done.5.back_1) | copy-start | bytes 98308
  108.7 5.0 %copy-start.6 = (bf16[16,1024]{1,0:T(8,128)(2,1)}, bf16[16,1024]{1,0:T(8,128)(2,1)S(1)}, u32[]{:S(2)}) copy-start(bf16[16,1024]{1,0:T(8,128)(2,1)S(1)} %collective-permute-done.6.back_2) | copy-start | bytes 98308
  113.7 0.6 copy-start.7
Sparse Core Ops, SparseCore 0:
  10.4 66.5 all-gather.1

commit v3 on v2

--- a/solution.py
+++ b/solution.py
@@ -64,7 +64,7 @@
 
 def edge_kernel(
     panels, nodes_in, halo_0, halo_1, halo_2, halo_3, edges_in, gain_in, send_row_in, recv_row_in, node_cot_in, edge_cot_in,
-    new_nodes, new_edges, grad_pre, own, out_0, out_1, out_2, out_3, grad_recv,
+    new_nodes, new_edges, grad_edges, own, out_0, out_1, out_2, out_3, part,
     w_send, w_recv, w_edge, w_out, table_rows, edges, gain, send_row, recv_row, node_cot, edge_cot,
     sems, small_sems,
 ):
@@ -78,20 +78,19 @@
     small = loads(first + rest, small_sems)
     order = ((w_send, SEND), (w_recv, RECEIVE), (w_edge, EDGE), (w_out, OUTPUT))
     copies = [fetches(panels, held, sems.at[i], which) for i, (held, which) in enumerate(order)]
-    begin(small[: len(first)])
+    begin(small)
     begin(copies[0])
-    begin(small[len(first) :])
-    for pair in copies[1:]:
-        begin(pair)
-    finish(small[: len(first)])
-    finish(copies[0])
-    lookup = dot(table_rows[...], matrix(w_send)).astype(BF)
-    finish(small[len(first) :])
+    begin(copies[1])
+    finish(small)
     to_recv = one_hot_t(recv_row[...], node_count)
     to_send = one_hot_t(send_row[...], table)
+    finish(copies[0])
+    begin(copies[2])
+    lookup = dot(table_rows[...], matrix(w_send)).astype(BF)
+    finish(copies[1])
+    begin(copies[3])
+    received = dot(table_rows[:node_count], matrix(w_recv)).astype(BF)
     grad_total = edge_cot[...].astype(F32) + picked(to_recv, node_cot[...])
-    finish(copies[1])
-    received = dot(table_rows[:node_count], matrix(w_recv)).astype(BF)
     finish(copies[2])
     preact = dot(edges[...], matrix(w_edge))
     preact = preact + picked(to_send, lookup)
@@ -112,34 +111,13 @@
     mean_along = jnp.mean(pulled * normal, axis=-1, keepdims=True)
     grad_projected = (scale * (pulled - mean_pulled - normal * mean_along)).astype(BF)
     grad_preact = (dot_rows(grad_projected, matrix(w_out)) * slope).astype(BF)
-    grad_pre[...] = grad_preact
     grad_lookup = dot(to_send, grad_preact)
     own[...] = grad_lookup[:node_count]
     for j, out in enumerate((out_0, out_1, out_2, out_3)):
         out[...] = grad_lookup[node_count + j * halo : node_count + (j + 1) * halo].astype(BF)
-    grad_recv[...] = dot(to_recv, grad_preact).astype(BF)
-
-
-def local_kernel(
-    panels, grad_pre_in, grad_recv_in, recv_row_in, node_cot_in, edge_cot_in, grad_edges, part,
-    w_edge, w_recv, grad_pre, grad_recv, recv_row, node_cot, edge_cot, sems, small_sems,
-):
-    small = loads(
-        ((grad_pre_in, grad_pre), (recv_row_in, recv_row), (node_cot_in, node_cot), (edge_cot_in, edge_cot),
-         (grad_recv_in, grad_recv)),
-        small_sems,
-    )
-    copies = [fetches(panels, w_edge, sems.at[0], EDGE), fetches(panels, w_recv, sems.at[1], RECEIVE)]
-    begin(copies[0])
-    begin(small)
-    begin(copies[1])
-    finish(small)
-    to_recv = one_hot_t(recv_row[...], node_cot.shape[0])
-    grad_total = edge_cot[...].astype(F32) + picked(to_recv, node_cot[...])
-    finish(copies[0])
-    grad_edges[...] = (grad_total + dot_rows(grad_pre[...], matrix(w_edge))).astype(BF)
-    finish(copies[1])
-    part[...] = node_cot[...].astype(F32) + dot_rows(grad_recv[...], matrix(w_recv))
+    grad_recv = dot(to_recv, grad_preact).astype(BF)
+    part[...] = node_cot[...].astype(F32) + dot_rows(grad_recv, matrix(w_recv))
+    grad_edges[...] = (grad_total + dot_rows(grad_preact, matrix(w_edge))).astype(BF)
 
 
 def node_kernel(
@@ -214,9 +192,9 @@
     arrived = [moved(chosen[j], shifts[j]) for j in range(2 * spread)]
     gain = norm_gain.reshape(1, -1)
     send_row, recv_row = senders.reshape(1, -1), receivers.reshape(1, -1)
-    new_nodes, new_edges, grad_pre, own, *outgoing, grad_recv = run(
+    new_nodes, new_edges, grad_edges, own, *outgoing, part = run(
         edge_kernel,
-        (rows(nodes), rows(edges), rows(edges), rows(nodes, F32), *halo_rows, rows(nodes)),
+        (rows(nodes), rows(edges), rows(edges), rows(nodes, F32), *halo_rows, rows(nodes, F32)),
         4,
         2 * 768 * width * width,
         panels,
@@ -224,10 +202,6 @@
         [rows(nodes + 2 * spread * halo), edge_states, gain, send_row, recv_row, node_cotangent, edge_cotangent],
     )
     back = [moved(outgoing[j], -shifts[j]) for j in range(2 * spread)]
-    near = [grad_pre, grad_recv, recv_row, node_cotangent, edge_cotangent]
-    grad_edges, part = run(
-        local_kernel, (rows(edges), rows(nodes, F32)), 2, 2 * 256 * width * width, panels, near, near
-    )
     last = [own, part, rows_by_shift, *back]
     grad_nodes = run(
         node_kernel, rows(nodes), 1, 2 * 64 * width * width, panels, last, last

time: 125 us -> 126 us (level)
  waiting for transfers between devices: 44.7 us -> 49.5 us
  Pallas kernels: 18.3 us -> 14.6 us
    ppermute x8, waiting for transfers between devices: 6.87 us -> 11.7 us  [moved(): lax.ppermute(value, AXES, [(i, (i + steps) % blocks) for i in range(block...]
    pallas_call x3 -> x2, Pallas kernels: 16.6 us -> 12.9 us  [run(): pl.pallas_call(kernel, out_shape=outs, in_specs=[HBM] * (1 + len(values))...]
  transfers between devices with their start and end apart: 9 -> 9, of which waited for: 3 -> 4; matrix products, arithmetic and copies ran while one was open for 0% -> 0% of each run, Pallas kernels for 5% -> 1%
where the time goes in v3:
time: 126 us
  waiting for transfers between devices  49.5 us (39%)
  starting transfers between devices  44.8 us (36%)
  Pallas kernels  14.6 us (12%)
  between operations  14.2 us (11%)
  other arithmetic  1.99 us (2%)
    ppermute x8, starting transfers between devices, moved(): lax.ppermute(value, AXES, [(i, (i + steps) % blocks) for i in range(block...  44.8 us
    all_gather x1, waiting for transfers between devices, shards(): lax.all_gather(mine.reshape(4 * panel, -1), ('core', 'mp'), axis=0, tiled...  37.8 us
    pallas_call x2, Pallas kernels, run(): pl.pallas_call(kernel, out_shape=outs, in_specs=[HBM] * (1 + len(values))...  12.9 us
    ppermute x8, waiting for transfers between devices, moved(): lax.ppermute(value, AXES, [(i, (i + steps) % blocks) for i in range(block...  11.7 us
  transfers between devices with their start and end apart: 9, of which 4 were waited for; matrix products, arithmetic and copies ran while one was open for 0% of the time, Pallas kernels for 1%

profile of v3, /device:TPU:8, one launch (start us, length us, event | category | flops | bytes accessed | tf_op | source)
XLA Modules:
  0.0 125.8 jit_solution(1732565961116116818)
XLA Ops:
  7.2 0.0 all-gather.2.cloned.1.call-start
  7.2 2.0 %fusion.2 = bf16[4,64,1024]{2,1,0:T(8,128)(2,1)} fusion(s32[]{:T(128)S(6)} %select_n.3, bf16[1,128,1024]{2,1,0:T(8,128)(2,1)} %bitcast.13, bf16[1,128,1024]{2,1,0:T(8,128)(2,1)} %bitcast.14, bf16[1,128,1024]{2,1,0:T(8,128)(2,1)} %bitcast.15, bf16[1,128,1024]{2,1,0:T(8,128)(2,1)} %bitcast.16), kind=kLoop, calls=%fused_computation.6 | loop fusion | flops 2097152 | bytes 1572868 | tf_op jit(solution)/shard_map/stack | solution.py:181
  9.2 0.0 all-gather.2.cloned.1.call-update
  9.2 1.8 %shard_map.147 = (bf16[16,1024]{1,0:T(8,128)(2,1)}, bf16[16,1024]{1,0:T(8,128)(2,1)}, bf16[16,1024]{1,0:T(8,128)(2,1)}, bf16[16,1024]{1,0:T(8,128)(2,1)}) custom-call(bf16[64,1024]{1,0:T(8,128)(2,1)} %nodes_in.1, s32[4,16]{1,0:T(4,128)} %bitcast.17), custom_call_target="tpu_custom_call" | custom-call | tf_op jit(solution)/shard_map/pallas_call | solution.py:191
  11.0 3.5 %collective-permute-start = (bf16[16,1024]{1,0:T(8,128)(2,1)}, bf16[16,1024]{1,0:T(8,128)(2,1)S(1)}, u32[]{:S(2)}, u32[]{:S(2)}) collective-permute-start(bf16[16,1024]{1,0:T(8,128)(2,1)} %get-tuple-element.17), channel_id=1, source_target_pairs={{0,1},{1,2},{2,3},{3,4},{4,5},{5,6},{6,7},{7,8},{8,9},{9,10},{10,1... | collective-permute-start | bytes 98312 | tf_op jit(solution)/shard_map/ppermute | solution.py:179
  14.5 5.7 %collective-permute-start.1 = (bf16[16,1024]{1,0:T(8,128)(2,1)}, bf16[16,1024]{1,0:T(8,128)(2,1)S(1)}, u32[]{:S(2)}, u32[]{:S(2)}) collective-permute-start(bf16[16,1024]{1,0:T(8,128)(2,1)} %get-tuple-element.18), channel_id=1, source_target_pairs={{0,2},{1,3},{2,4},{3,5},{4,6},{5,7},{6,8},{7,9},{8,10},{9,11},{10,... | collective-permute-start | bytes 98312 | tf_op jit(solution)/shard_map/ppermute | solution.py:179
  20.2 6.0 %collective-permute-start.2 = (bf16[16,1024]{1,0:T(8,128)(2,1)}, bf16[16,1024]{1,0:T(8,128)(2,1)S(1)}, u32[]{:S(2)}, u32[]{:S(2)}) collective-permute-start(bf16[16,1024]{1,0:T(8,128)(2,1)} %get-tuple-element.19), channel_id=1, source_target_pairs={{0,767},{1,0},{2,1},{3,2},{4,3},{5,4},{6,5},{7,6},{8,7},{9,8},{10,... | collective-permute-start | bytes 98312 | tf_op jit(solution)/shard_map/ppermute | solution.py:179
  26.2 11.0 %collective-permute-start.3 = (bf16[16,1024]{1,0:T(8,128)(2,1)}, bf16[16,1024]{1,0:T(8,128)(2,1)S(1)}, u32[]{:S(2)}, u32[]{:S(2)}) collective-permute-start(bf16[16,1024]{1,0:T(8,128)(2,1)} %get-tuple-element.20), channel_id=1, source_target_pairs={{0,766},{1,767},{2,0},{3,1},{4,2},{5,3},{6,4},{7,5},{8,6},{9,7},{1... | collective-permute-start | bytes 98312 | tf_op jit(solution)/shard_map/ppermute | solution.py:179
  37.2 0.0 collective-permute-done.halo_0
  37.2 0.0 copy-start
  37.3 0.0 collective-permute-done.1.halo_1
  37.3 0.0 collective-permute-done.2.halo_2
  37.3 1.8 %collective-permute-done.3.halo_3 = bf16[16,1024]{1,0:T(8,128)(2,1)S(1)} collective-permute-done((bf16[16,1024]{1,0:T(8,128)(2,1)}, bf16[16,1024]{1,0:T(8,128)(2,1)S(1)}, u32[]{:S(2)}, u32[]{:S(2)}) %collective-permute-start.3) | collective-permute-done | bytes 32800 | tf_op jit(solution)/shard_map/ppermute | solution.py:179
  39.1 37.8 %all-gather.2.cloned.1.call-done = bf16[4096,1024]{1,0:T(8,128)(2,1)} async-done(((bf16[256,1024]{1,0:T(8,128)(2,1)}), bf16[4096,1024]{1,0:T(8,128)(2,1)}) %all-gather.2.cloned.1.call-update) | async-done | bytes 8388624 | tf_op jit(solution)/shard_map/all_gather | solution.py:183
  77.0 9.3 %shard_map.148 = (bf16[64,1024]{1,0:T(8,128)(2,1)}, bf16[192,1024]{1,0:T(8,128)(2,1)}, bf16[192,1024]{1,0:T(8,128)(2,1)}, f32[64,1024]{1,0:T(8,128)}, bf16[16,10...) custom-call(bf16[2,8,4,64,1024]{4,3,2,1,0:T(8,128)(2,1)} %bitcast.10, ...), custom_call_target="tpu_custom_call" | custom-call | flops 1610612736 | bytes 4194304 | tf_op jit(solution)/shard_map/pallas_call | solution.py:142
  86.3 3.5 %collective-permute-start.4 = (bf16[16,1024]{1,0:T(8,128)(2,1)}, bf16[16,1024]{1,0:T(8,128)(2,1)S(1)}, u32[]{:S(2)}, u32[]{:S(2)}) collective-permute-start(bf16[16,1024]{1,0:T(8,128)(2,1)} %get-tuple-element.25), channel_id=1, source_target_pairs={{0,767},{1,0},{2,1},{3,2},{4,3},{5,4},{6,5},{7,6},{8,7},{9,8},{10,... | collective-permute-start | bytes 98312 | tf_op jit(solution)/shard_map/ppermute | solution.py:179
  89.9 10.0 %collective-permute-start.5 = (bf16[16,1024]{1,0:T(8,128)(2,1)}, bf16[16,1024]{1,0:T(8,128)(2,1)S(1)}, u32[]{:S(2)}, u32[]{:S(2)}) collective-permute-start(bf16[16,1024]{1,0:T(8,128)(2,1)} %get-tuple-element.26), channel_id=1, source_target_pairs={{0,766},{1,767},{2,0},{3,1},{4,2},{5,3},{6,4},{7,5},{8,6},{9,7},{1... | collective-permute-start | bytes 98312 | tf_op jit(solution)/shard_map/ppermute | solution.py:179
  99.9 3.1 %collective-permute-start.6 = (bf16[16,1024]{1,0:T(8,128)(2,1)}, bf16[16,1024]{1,0:T(8,128)(2,1)S(1)}, u32[]{:S(2)}, u32[]{:S(2)}) collective-permute-start(bf16[16,1024]{1,0:T(8,128)(2,1)} %get-tuple-element.27), channel_id=1, source_target_pairs={{0,1},{1,2},{2,3},{3,4},{4,5},{5,6},{6,7},{7,8},{8,9},{9,10},{10,1... | collective-permute-start | bytes 98312 | tf_op jit(solution)/shard_map/ppermute | solution.py:179
  103.0 1.9 %collective-permute-start.7 = (bf16[16,1024]{1,0:T(8,128)(2,1)}, bf16[16,1024]{1,0:T(8,128)(2,1)S(1)}, u32[]{:S(2)}, u32[]{:S(2)}) collective-permute-start(bf16[16,1024]{1,0:T(8,128)(2,1)} %get-tuple-element.28), channel_id=1, source_target_pairs={{0,2},{1,3},{2,4},{3,5},{4,6},{5,7},{6,8},{7,9},{8,10},{9,11},{10,... | collective-permute-start | bytes 98312 | tf_op jit(solution)/shard_map/ppermute | solution.py:179
  104.9 0.0 collective-permute-done.4.back_0
  105.0 1.0 collective-permute-done.6.back_2
  106.0 8.8 %collective-permute-done.7.back_3 = bf16[16,1024]{1,0:T(8,128)(2,1)S(1)} collective-permute-done((bf16[16,1024]{1,0:T(8,128)(2,1)}, bf16[16,1024]{1,0:T(8,128)(2,1)S(1)}, u32[]{:S(2)}, u32[]{:S(2)}) %collective-permute-start.7) | collective-permute-done | bytes 32800 | tf_op jit(solution)/shard_map/ppermute | solution.py:179
  114.8 0.6 copy-done.7
  115.4 3.5 %shard_map.149 = bf16[64,1024]{1,0:T(8,128)(2,1)} custom-call(bf16[2,8,4,64,1024]{4,3,2,1,0:T(8,128)(2,1)} %bitcast.11, f32[64,1024]{1,0:T(8,128)} %get-tuple-element.23.own_in, f32[64,1024]{1,0:T(8,128)} %get-tuple-element.24.part_in, s32[4,16]{1,0:T(4,128)} %bitcast.18, bf16[16,1024]{1,0:T(8,128)(2,1)} %copy-done.4, bf16[16,1024]{1,0:T(8,128)(2,1)} %copy-done.5, ...), custom_call_target="tpu_custom_call" | custom-call | flops 134217728 | bytes 4194304 | tf_op jit(solution)/shard_map/pallas_call | solution.py:142
  (15 shorter events, 0.0 us)
Async XLA Ops:
  7.2 69.8 %all-gather.2.cloned.1.call-start = ((), (), s32[]{:S(2)}) async-start(), calls=%async_computation | async-start | bytes 8912896 | tf_op jit(solution)/shard_map/all_gather | solution.py:183
  11.0 26.2 %collective-permute-start = (bf16[16,1024]{1,0:T(8,128)(2,1)}, bf16[16,1024]{1,0:T(8,128)(2,1)S(1)}, u32[]{:S(2)}, u32[]{:S(2)}) collective-permute-start(bf16[16,1024]{1,0:T(8,128)(2,1)} %get-tuple-element.17), channel_id=1, source_target_pairs={{0,1},{1,2},{2,3},{3,4},{4,5},{5,6},{6,7},{7,8},{8,9},{9,10},{10,1... | collective-permute-start | bytes 98312 | tf_op jit(solution)/shard_map/ppermute | solution.py:179
  14.5 22.8 %collective-permute-start.1 = (bf16[16,1024]{1,0:T(8,128)(2,1)}, bf16[16,1024]{1,0:T(8,128)(2,1)S(1)}, u32[]{:S(2)}, u32[]{:S(2)}) collective-permute-start(bf16[16,1024]{1,0:T(8,128)(2,1)} %get-tuple-element.18), channel_id=1, source_target_pairs={{0,2},{1,3},{2,4},{3,5},{4,6},{5,7},{6,8},{7,9},{8,10},{9,11},{10,... | collective-permute-start | bytes 98312 | tf_op jit(solution)/shard_map/ppermute | solution.py:179
  20.2 17.1 %collective-permute-start.2 = (bf16[16,1024]{1,0:T(8,128)(2,1)}, bf16[16,1024]{1,0:T(8,128)(2,1)S(1)}, u32[]{:S(2)}, u32[]{:S(2)}) collective-permute-start(bf16[16,1024]{1,0:T(8,128)(2,1)} %get-tuple-element.19), channel_id=1, source_target_pairs={{0,767},{1,0},{2,1},{3,2},{4,3},{5,4},{6,5},{7,6},{8,7},{9,8},{10,... | collective-permute-start | bytes 98312 | tf_op jit(solution)/shard_map/ppermute | solution.py:179
  26.2 12.9 %collective-permute-start.3 = (bf16[16,1024]{1,0:T(8,128)(2,1)}, bf16[16,1024]{1,0:T(8,128)(2,1)S(1)}, u32[]{:S(2)}, u32[]{:S(2)}) collective-permute-start(bf16[16,1024]{1,0:T(8,128)(2,1)} %get-tuple-element.20), channel_id=1, source_target_pairs={{0,766},{1,767},{2,0},{3,1},{4,2},{5,3},{6,4},{7,5},{8,6},{9,7},{1... | collective-permute-start | bytes 98312 | tf_op jit(solution)/shard_map/ppermute | solution.py:179
  37.2 39.7 %copy-start = (bf16[16,1024]{1,0:T(8,128)(2,1)}, bf16[16,1024]{1,0:T(8,128)(2,1)S(1)}, u32[]{:S(2)}) copy-start(bf16[16,1024]{1,0:T(8,128)(2,1)S(1)} %collective-permute-done.halo_0) | copy-start | bytes 98308
  37.3 39.7 %copy-start.1 = (bf16[16,1024]{1,0:T(8,128)(2,1)}, bf16[16,1024]{1,0:T(8,128)(2,1)S(1)}, u32[]{:S(2)}) copy-start(bf16[16,1024]{1,0:T(8,128)(2,1)S(1)} %collective-permute-done.1.halo_1) | copy-start | bytes 98308
  37.3 39.7 %copy-start.2 = (bf16[16,1024]{1,0:T(8,128)(2,1)}, bf16[16,1024]{1,0:T(8,128)(2,1)S(1)}, u32[]{:S(2)}) copy-start(bf16[16,1024]{1,0:T(8,128)(2,1)S(1)} %collective-permute-done.2.halo_2) | copy-start | bytes 98308
  39.1 37.9 %copy-start.3 = (bf16[16,1024]{1,0:T(8,128)(2,1)}, bf16[16,1024]{1,0:T(8,128)(2,1)S(1)}, u32[]{:S(2)}) copy-start(bf16[16,1024]{1,0:T(8,128)(2,1)S(1)} %collective-permute-done.3.halo_3) | copy-start | bytes 98308
  86.3 18.6 %collective-permute-start.4 = (bf16[16,1024]{1,0:T(8,128)(2,1)}, bf16[16,1024]{1,0:T(8,128)(2,1)S(1)}, u32[]{:S(2)}, u32[]{:S(2)}) collective-permute-start(bf16[16,1024]{1,0:T(8,128)(2,1)} %get-tuple-element.25), channel_id=1, source_target_pairs={{0,767},{1,0},{2,1},{3,2},{4,3},{5,4},{6,5},{7,6},{8,7},{9,8},{10,... | collective-permute-start | bytes 98312 | tf_op jit(solution)/shard_map/ppermute | solution.py:179
  89.9 15.1 %collective-permute-start.5 = (bf16[16,1024]{1,0:T(8,128)(2,1)}, bf16[16,1024]{1,0:T(8,128)(2,1)S(1)}, u32[]{:S(2)}, u32[]{:S(2)}) collective-permute-start(bf16[16,1024]{1,0:T(8,128)(2,1)} %get-tuple-element.26), channel_id=1, source_target_pairs={{0,766},{1,767},{2,0},{3,1},{4,2},{5,3},{6,4},{7,5},{8,6},{9,7},{1... | collective-permute-start | bytes 98312 | tf_op jit(solution)/shard_map/ppermute | solution.py:179
  99.9 6.1 %collective-permute-start.6 = (bf16[16,1024]{1,0:T(8,128)(2,1)}, bf16[16,1024]{1,0:T(8,128)(2,1)S(1)}, u32[]{:S(2)}, u32[]{:S(2)}) collective-permute-start(bf16[16,1024]{1,0:T(8,128)(2,1)} %get-tuple-element.27), channel_id=1, source_target_pairs={{0,1},{1,2},{2,3},{3,4},{4,5},{5,6},{6,7},{7,8},{8,9},{9,10},{10,1... | collective-permute-start | bytes 98312 | tf_op jit(solution)/shard_map/ppermute | solution.py:179
  103.0 11.8 %collective-permute-start.7 = (bf16[16,1024]{1,0:T(8,128)(2,1)}, bf16[16,1024]{1,0:T(8,128)(2,1)S(1)}, u32[]{:S(2)}, u32[]{:S(2)}) collective-permute-start(bf16[16,1024]{1,0:T(8,128)(2,1)} %get-tuple-element.28), channel_id=1, source_target_pairs={{0,2},{1,3},{2,4},{3,5},{4,6},{5,7},{6,8},{7,9},{8,10},{9,11},{10,... | collective-permute-start | bytes 98312 | tf_op jit(solution)/shard_map/ppermute | solution.py:179
  104.9 9.9 %copy-start.4 = (bf16[16,1024]{1,0:T(8,128)(2,1)}, bf16[16,1024]{1,0:T(8,128)(2,1)S(1)}, u32[]{:S(2)}) copy-start(bf16[16,1024]{1,0:T(8,128)(2,1)S(1)} %collective-permute-done.4.back_0) | copy-start | bytes 98308
  105.0 9.9 %copy-start.5 = (bf16[16,1024]{1,0:T(8,128)(2,1)}, bf16[16,1024]{1,0:T(8,128)(2,1)S(1)}, u32[]{:S(2)}) copy-start(bf16[16,1024]{1,0:T(8,128)(2,1)S(1)} %collective-permute-done.5.back_1) | copy-start | bytes 98308
  106.0 8.8 %copy-start.6 = (bf16[16,1024]{1,0:T(8,128)(2,1)}, bf16[16,1024]{1,0:T(8,128)(2,1)S(1)}, u32[]{:S(2)}) copy-start(bf16[16,1024]{1,0:T(8,128)(2,1)S(1)} %collective-permute-done.6.back_2) | copy-start | bytes 98308
  114.8 0.6 copy-start.7
Sparse Core Ops, SparseCore 0:
  10.4 66.5 all-gather.1

commit v4 on v2

--- a/solution.py
+++ b/solution.py
@@ -1,3 +1,5 @@
+import functools
+
 import jax
 import jax.numpy as jnp
 from jax import lax
@@ -78,20 +80,19 @@
     small = loads(first + rest, small_sems)
     order = ((w_send, SEND), (w_recv, RECEIVE), (w_edge, EDGE), (w_out, OUTPUT))
     copies = [fetches(panels, held, sems.at[i], which) for i, (held, which) in enumerate(order)]
-    begin(small[: len(first)])
+    begin(small)
     begin(copies[0])
-    begin(small[len(first) :])
-    for pair in copies[1:]:
-        begin(pair)
-    finish(small[: len(first)])
-    finish(copies[0])
-    lookup = dot(table_rows[...], matrix(w_send)).astype(BF)
-    finish(small[len(first) :])
+    begin(copies[1])
+    finish(small)
     to_recv = one_hot_t(recv_row[...], node_count)
     to_send = one_hot_t(send_row[...], table)
+    finish(copies[0])
+    begin(copies[2])
+    lookup = dot(table_rows[...], matrix(w_send)).astype(BF)
+    finish(copies[1])
+    begin(copies[3])
+    received = dot(table_rows[:node_count], matrix(w_recv)).astype(BF)
     grad_total = edge_cot[...].astype(F32) + picked(to_recv, node_cot[...])
-    finish(copies[1])
-    received = dot(table_rows[:node_count], matrix(w_recv)).astype(BF)
     finish(copies[2])
     preact = dot(edges[...], matrix(w_edge))
     preact = preact + picked(to_send, lookup)
@@ -143,7 +144,7 @@
 
 
 def node_kernel(
-    panels, own_in, part_in, rows_in, back_0, back_1, back_2, back_3, grad_nodes,
+    order, panels, own_in, part_in, rows_in, back_0, back_1, back_2, back_3, grad_nodes,
     w_send, own, part, rows, b_0, b_1, b_2, b_3, sems, small_sems,
 ):
     ins = (back_0, back_1, back_2, back_3, rows_in, own_in, part_in)
@@ -153,7 +154,7 @@
     begin(small)
     finish(small)
     grad_send = own[...]
-    for j, back in enumerate((b_0, b_1, b_2, b_3)):
+    for j, back in zip(order, (b_0, b_1, b_2, b_3)):
         grad_send = grad_send + dot(one_hot_t(rows[j : j + 1], own.shape[0]), back[...])
     finish(copies)
     grad_nodes[...] = (part[...] + dot_rows(grad_send.astype(BF), matrix(w_send))).astype(BF)
@@ -223,14 +224,15 @@
         [node_states, *arrived, edge_states, gain, send_row, recv_row, node_cotangent, edge_cotangent],
         [rows(nodes + 2 * spread * halo), edge_states, gain, send_row, recv_row, node_cotangent, edge_cotangent],
     )
-    back = [moved(outgoing[j], -shifts[j]) for j in range(2 * spread)]
+    order = sorted(range(2 * spread), key=lambda j: (shifts[j] > 0, shifts[j]))
+    back = [moved(outgoing[j], -shifts[j]) for j in order]
     near = [grad_pre, grad_recv, recv_row, node_cotangent, edge_cotangent]
     grad_edges, part = run(
         local_kernel, (rows(edges), rows(nodes, F32)), 2, 2 * 256 * width * width, panels, near, near
     )
     last = [own, part, rows_by_shift, *back]
     grad_nodes = run(
-        node_kernel, rows(nodes), 1, 2 * 64 * width * width, panels, last, last
+        functools.partial(node_kernel, order), rows(nodes), 1, 2 * 64 * width * width, panels, last, last
     )
     return new_nodes, new_edges, grad_nodes, grad_edges
 

time: 125 us -> 119 us (0.952)
  waiting for transfers between devices: 44.7 us -> 39.7 us
    ppermute x8, waiting for transfers between devices: 6.87 us -> 1.85 us  [moved(): lax.ppermute(value, AXES, [(i, (i + steps) % blocks) for i in range(block...]
  transfers between devices with their start and end apart: 9 -> 9, of which waited for: 3 -> 2; matrix products, arithmetic and copies ran while one was open for 0% -> 0% of each run, Pallas kernels for 5% -> 6%
where the time goes in v4:
time: 119 us
  starting transfers between devices  44.2 us (37%)
  waiting for transfers between devices  39.7 us (33%)
  Pallas kernels  18 us (15%)
  between operations  14.2 us (12%)
  other arithmetic  1.98 us (2%)
    ppermute x8, starting transfers between devices, moved(): lax.ppermute(value, AXES, [(i, (i + steps) % blocks) for i in range(block...  44.2 us
    all_gather x1, waiting for transfers between devices, shards(): lax.all_gather(mine.reshape(4 * panel, -1), ('core', 'mp'), axis=0, tiled...  37.9 us
    pallas_call x3, Pallas kernels, run(): pl.pallas_call(kernel, out_shape=outs, in_specs=[HBM] * (1 + len(values))...  16.3 us
  transfers between devices with their start and end apart: 9, of which 2 were waited for; matrix products, arithmetic and copies ran while one was open for 0% of the time, Pallas kernels for 6%

profile of v4, /device:TPU:8, one launch (start us, length us, event | category | flops | bytes accessed | tf_op | source)
XLA Modules:
  0.0 118.8 jit_solution(4407514375850550471)
XLA Ops:
  7.2 0.0 all-gather.2.cloned.1.call-start
  7.2 2.0 %fusion.2 = bf16[4,64,1024]{2,1,0:T(8,128)(2,1)} fusion(s32[]{:T(128)S(6)} %select_n.3, bf16[1,128,1024]{2,1,0:T(8,128)(2,1)} %bitcast.14, bf16[1,128,1024]{2,1,0:T(8,128)(2,1)} %bitcast.15, bf16[1,128,1024]{2,1,0:T(8,128)(2,1)} %bitcast.16, bf16[1,128,1024]{2,1,0:T(8,128)(2,1)} %bitcast.17), kind=kLoop, calls=%fused_computation.6 | loop fusion | flops 2097152 | bytes 1572868 | tf_op jit(solution)/shard_map/stack | solution.py:204
  9.2 0.0 all-gather.2.cloned.1.call-update
  9.2 1.8 %shard_map.147 = (bf16[16,1024]{1,0:T(8,128)(2,1)}, bf16[16,1024]{1,0:T(8,128)(2,1)}, bf16[16,1024]{1,0:T(8,128)(2,1)}, bf16[16,1024]{1,0:T(8,128)(2,1)}) custom-call(bf16[64,1024]{1,0:T(8,128)(2,1)} %nodes_in.1, s32[4,16]{1,0:T(4,128)} %bitcast.18), custom_call_target="tpu_custom_call" | custom-call | tf_op jit(solution)/shard_map/pallas_call | solution.py:214
  11.0 3.5 %collective-permute-start = (bf16[16,1024]{1,0:T(8,128)(2,1)}, bf16[16,1024]{1,0:T(8,128)(2,1)S(1)}, u32[]{:S(2)}, u32[]{:S(2)}) collective-permute-start(bf16[16,1024]{1,0:T(8,128)(2,1)} %get-tuple-element.19), channel_id=1, source_target_pairs={{0,1},{1,2},{2,3},{3,4},{4,5},{5,6},{6,7},{7,8},{8,9},{9,10},{10,1... | collective-permute-start | bytes 98312 | tf_op jit(solution)/shard_map/ppermute | solution.py:202
  14.5 5.7 %collective-permute-start.1 = (bf16[16,1024]{1,0:T(8,128)(2,1)}, bf16[16,1024]{1,0:T(8,128)(2,1)S(1)}, u32[]{:S(2)}, u32[]{:S(2)}) collective-permute-start(bf16[16,1024]{1,0:T(8,128)(2,1)} %get-tuple-element.20), channel_id=1, source_target_pairs={{0,2},{1,3},{2,4},{3,5},{4,6},{5,7},{6,8},{7,9},{8,10},{9,11},{10,... | collective-permute-start | bytes 98312 | tf_op jit(solution)/shard_map/ppermute | solution.py:202
  20.2 6.0 %collective-permute-start.2 = (bf16[16,1024]{1,0:T(8,128)(2,1)}, bf16[16,1024]{1,0:T(8,128)(2,1)S(1)}, u32[]{:S(2)}, u32[]{:S(2)}) collective-permute-start(bf16[16,1024]{1,0:T(8,128)(2,1)} %get-tuple-element.21), channel_id=1, source_target_pairs={{0,767},{1,0},{2,1},{3,2},{4,3},{5,4},{6,5},{7,6},{8,7},{9,8},{10,... | collective-permute-start | bytes 98312 | tf_op jit(solution)/shard_map/ppermute | solution.py:202
  26.2 11.0 %collective-permute-start.3 = (bf16[16,1024]{1,0:T(8,128)(2,1)}, bf16[16,1024]{1,0:T(8,128)(2,1)S(1)}, u32[]{:S(2)}, u32[]{:S(2)}) collective-permute-start(bf16[16,1024]{1,0:T(8,128)(2,1)} %get-tuple-element.22), channel_id=1, source_target_pairs={{0,766},{1,767},{2,0},{3,1},{4,2},{5,3},{6,4},{7,5},{8,6},{9,7},{1... | collective-permute-start | bytes 98312 | tf_op jit(solution)/shard_map/ppermute | solution.py:202
  37.2 0.0 collective-permute-done.halo_0
  37.2 0.0 collective-permute-done.1.halo_1
  37.3 0.0 copy-start.2
  37.3 1.8 %collective-permute-done.3.halo_3 = bf16[16,1024]{1,0:T(8,128)(2,1)S(1)} collective-permute-done((bf16[16,1024]{1,0:T(8,128)(2,1)}, bf16[16,1024]{1,0:T(8,128)(2,1)S(1)}, u32[]{:S(2)}, u32[]{:S(2)}) %collective-permute-start.3) | collective-permute-done | bytes 32800 | tf_op jit(solution)/shard_map/ppermute | solution.py:202
  39.1 37.9 %all-gather.2.cloned.1.call-done = bf16[4096,1024]{1,0:T(8,128)(2,1)} async-done(((bf16[256,1024]{1,0:T(8,128)(2,1)}), bf16[4096,1024]{1,0:T(8,128)(2,1)}) %all-gather.2.cloned.1.call-update) | async-done | bytes 8388624 | tf_op jit(solution)/shard_map/all_gather | solution.py:206
  77.0 8.0 %shard_map.148 = (bf16[64,1024]{1,0:T(8,128)(2,1)}, bf16[192,1024]{1,0:T(8,128)(2,1)}, bf16[192,1024]{1,0:T(8,128)(2,1)}, f32[64,1024]{1,0:T(8,128)}, bf16[16,10...) custom-call(bf16[2,8,4,64,1024]{4,3,2,1,0:T(8,128)(2,1)} %bitcast.10, ...), custom_call_target="tpu_custom_call" | custom-call | flops 1610612736 | bytes 4194304 | tf_op jit(solution)/shard_map/pallas_call | solution.py:165
  85.0 5.2 %collective-permute-start.4 = (bf16[16,1024]{1,0:T(8,128)(2,1)}, bf16[16,1024]{1,0:T(8,128)(2,1)S(1)}, u32[]{:S(2)}, u32[]{:S(2)}) collective-permute-start(bf16[16,1024]{1,0:T(8,128)(2,1)} %get-tuple-element.29), channel_id=1, source_target_pairs={{0,2},{1,3},{2,4},{3,5},{4,6},{5,7},{6,8},{7,9},{8,10},{9,11},{10,... | collective-permute-start | bytes 98312 | tf_op jit(solution)/shard_map/ppermute | solution.py:202
  90.1 2.5 %collective-permute-start.5 = (bf16[16,1024]{1,0:T(8,128)(2,1)}, bf16[16,1024]{1,0:T(8,128)(2,1)S(1)}, u32[]{:S(2)}, u32[]{:S(2)}) collective-permute-start(bf16[16,1024]{1,0:T(8,128)(2,1)} %get-tuple-element.30), channel_id=1, source_target_pairs={{0,1},{1,2},{2,3},{3,4},{4,5},{5,6},{6,7},{7,8},{8,9},{9,10},{10,1... | collective-permute-start | bytes 98312 | tf_op jit(solution)/shard_map/ppermute | solution.py:202
  92.7 3.3 %collective-permute-start.6 = (bf16[16,1024]{1,0:T(8,128)(2,1)}, bf16[16,1024]{1,0:T(8,128)(2,1)S(1)}, u32[]{:S(2)}, u32[]{:S(2)}) collective-permute-start(bf16[16,1024]{1,0:T(8,128)(2,1)} %get-tuple-element.31), channel_id=1, source_target_pairs={{0,767},{1,0},{2,1},{3,2},{4,3},{5,4},{6,5},{7,6},{8,7},{9,8},{10,... | collective-permute-start | bytes 98312 | tf_op jit(solution)/shard_map/ppermute | solution.py:202
  96.0 7.0 %collective-permute-start.7 = (bf16[16,1024]{1,0:T(8,128)(2,1)}, bf16[16,1024]{1,0:T(8,128)(2,1)S(1)}, u32[]{:S(2)}, u32[]{:S(2)}) collective-permute-start(bf16[16,1024]{1,0:T(8,128)(2,1)} %get-tuple-element.32), channel_id=1, source_target_pairs={{0,766},{1,767},{2,0},{3,1},{4,2},{5,3},{6,4},{7,5},{8,6},{9,7},{1... | collective-permute-start | bytes 98312 | tf_op jit(solution)/shard_map/ppermute | solution.py:202
  103.0 4.8 %shard_map.149 = (bf16[192,1024]{1,0:T(8,128)(2,1)}, f32[64,1024]{1,0:T(8,128)}) custom-call(bf16[2,8,4,64,1024]{4,3,2,1,0:T(8,128)(2,1)} %bitcast.11, bf16[192,1024]{1,0:T(8,128)(2,1)} %get-tuple-element.26.grad_pre_in, bf16[64,1024]{1,0:T(8,128)(2,1)} %get-tuple-element.27.grad_recv_in, s32[1,192]{1,0:T(1,128)} %bitcast.22, bf16[64,1024]{1,0:T(8,128)(2,1)} %node_cot_in.3, ...), custom_call_target="tpu_custom_call" | custom-call | flops 536870912 | bytes 4194304 | tf_op jit(solution)/shard_map/pallas_call | solution.py:165
  107.8 0.5 copy-done.3
  108.4 0.0 copy-done.5
  108.4 0.0 copy-done.6
  108.4 0.0 copy-done.7
  108.4 3.5 %shard_map.150 = bf16[64,1024]{1,0:T(8,128)(2,1)} custom-call(bf16[2,8,4,64,1024]{4,3,2,1,0:T(8,128)(2,1)} %bitcast.12, f32[64,1024]{1,0:T(8,128)} %get-tuple-element.25.own_in, f32[64,1024]{1,0:T(8,128)} %get-tuple-element.28.part_in, s32[4,16]{1,0:T(4,128)} %bitcast.19, bf16[16,1024]{1,0:T(8,128)(2,1)} %copy-done.3, bf16[16,1024]{1,0:T(8,128)(2,1)} %copy-done.5, ...), custom_call_target="tpu_custom_call" | custom-call | flops 134217728 | bytes 4194304 | tf_op jit(solution)/shard_map/pallas_call | solution.py:165
  (16 shorter events, 0.0 us)
Async XLA Ops:
  7.2 69.8 %all-gather.2.cloned.1.call-start = ((), (), s32[]{:S(2)}) async-start(), calls=%async_computation | async-start | bytes 8912896 | tf_op jit(solution)/shard_map/all_gather | solution.py:206
  11.0 26.2 %collective-permute-start = (bf16[16,1024]{1,0:T(8,128)(2,1)}, bf16[16,1024]{1,0:T(8,128)(2,1)S(1)}, u32[]{:S(2)}, u32[]{:S(2)}) collective-permute-start(bf16[16,1024]{1,0:T(8,128)(2,1)} %get-tuple-element.19), channel_id=1, source_target_pairs={{0,1},{1,2},{2,3},{3,4},{4,5},{5,6},{6,7},{7,8},{8,9},{9,10},{10,1... | collective-permute-start | bytes 98312 | tf_op jit(solution)/shard_map/ppermute | solution.py:202
  14.5 22.8 %collective-permute-start.1 = (bf16[16,1024]{1,0:T(8,128)(2,1)}, bf16[16,1024]{1,0:T(8,128)(2,1)S(1)}, u32[]{:S(2)}, u32[]{:S(2)}) collective-permute-start(bf16[16,1024]{1,0:T(8,128)(2,1)} %get-tuple-element.20), channel_id=1, source_target_pairs={{0,2},{1,3},{2,4},{3,5},{4,6},{5,7},{6,8},{7,9},{8,10},{9,11},{10,... | collective-permute-start | bytes 98312 | tf_op jit(solution)/shard_map/ppermute | solution.py:202
  20.2 17.1 %collective-permute-start.2 = (bf16[16,1024]{1,0:T(8,128)(2,1)}, bf16[16,1024]{1,0:T(8,128)(2,1)S(1)}, u32[]{:S(2)}, u32[]{:S(2)}) collective-permute-start(bf16[16,1024]{1,0:T(8,128)(2,1)} %get-tuple-element.21), channel_id=1, source_target_pairs={{0,767},{1,0},{2,1},{3,2},{4,3},{5,4},{6,5},{7,6},{8,7},{9,8},{10,... | collective-permute-start | bytes 98312 | tf_op jit(solution)/shard_map/ppermute | solution.py:202
  26.2 12.9 %collective-permute-start.3 = (bf16[16,1024]{1,0:T(8,128)(2,1)}, bf16[16,1024]{1,0:T(8,128)(2,1)S(1)}, u32[]{:S(2)}, u32[]{:S(2)}) collective-permute-start(bf16[16,1024]{1,0:T(8,128)(2,1)} %get-tuple-element.22), channel_id=1, source_target_pairs={{0,766},{1,767},{2,0},{3,1},{4,2},{5,3},{6,4},{7,5},{8,6},{9,7},{1... | collective-permute-start | bytes 98312 | tf_op jit(solution)/shard_map/ppermute | solution.py:202
  37.2 39.7 %copy-start = (bf16[16,1024]{1,0:T(8,128)(2,1)}, bf16[16,1024]{1,0:T(8,128)(2,1)S(1)}, u32[]{:S(2)}) copy-start(bf16[16,1024]{1,0:T(8,128)(2,1)S(1)} %collective-permute-done.halo_0) | copy-start | bytes 98308
  37.3 39.7 %copy-start.1 = (bf16[16,1024]{1,0:T(8,128)(2,1)}, bf16[16,1024]{1,0:T(8,128)(2,1)S(1)}, u32[]{:S(2)}) copy-start(bf16[16,1024]{1,0:T(8,128)(2,1)S(1)} %collective-permute-done.1.halo_1) | copy-start | bytes 98308
  37.3 39.7 %copy-start.2 = (bf16[16,1024]{1,0:T(8,128)(2,1)}, bf16[16,1024]{1,0:T(8,128)(2,1)S(1)}, u32[]{:S(2)}) copy-start(bf16[16,1024]{1,0:T(8,128)(2,1)S(1)} %collective-permute-done.2.halo_2) | copy-start | bytes 98308
  39.1 37.9 %copy-start.4 = (bf16[16,1024]{1,0:T(8,128)(2,1)}, bf16[16,1024]{1,0:T(8,128)(2,1)S(1)}, u32[]{:S(2)}) copy-start(bf16[16,1024]{1,0:T(8,128)(2,1)S(1)} %collective-permute-done.3.halo_3) | copy-start | bytes 98308
  85.0 22.8 %collective-permute-start.4 = (bf16[16,1024]{1,0:T(8,128)(2,1)}, bf16[16,1024]{1,0:T(8,128)(2,1)S(1)}, u32[]{:S(2)}, u32[]{:S(2)}) collective-permute-start(bf16[16,1024]{1,0:T(8,128)(2,1)} %get-tuple-element.29), channel_id=1, source_target_pairs={{0,2},{1,3},{2,4},{3,5},{4,6},{5,7},{6,8},{7,9},{8,10},{9,11},{10,... | collective-permute-start | bytes 98312 | tf_op jit(solution)/shard_map/ppermute | solution.py:202
  90.1 17.6 %collective-permute-start.5 = (bf16[16,1024]{1,0:T(8,128)(2,1)}, bf16[16,1024]{1,0:T(8,128)(2,1)S(1)}, u32[]{:S(2)}, u32[]{:S(2)}) collective-permute-start(bf16[16,1024]{1,0:T(8,128)(2,1)} %get-tuple-element.30), channel_id=1, source_target_pairs={{0,1},{1,2},{2,3},{3,4},{4,5},{5,6},{6,7},{7,8},{8,9},{9,10},{10,1... | collective-permute-start | bytes 98312 | tf_op jit(solution)/shard_map/ppermute | solution.py:202
  92.7 15.1 %collective-permute-start.6 = (bf16[16,1024]{1,0:T(8,128)(2,1)}, bf16[16,1024]{1,0:T(8,128)(2,1)S(1)}, u32[]{:S(2)}, u32[]{:S(2)}) collective-permute-start(bf16[16,1024]{1,0:T(8,128)(2,1)} %get-tuple-element.31), channel_id=1, source_target_pairs={{0,767},{1,0},{2,1},{3,2},{4,3},{5,4},{6,5},{7,6},{8,7},{9,8},{10,... | collective-permute-start | bytes 98312 | tf_op jit(solution)/shard_map/ppermute | solution.py:202
  96.0 11.8 %collective-permute-start.7 = (bf16[16,1024]{1,0:T(8,128)(2,1)}, bf16[16,1024]{1,0:T(8,128)(2,1)S(1)}, u32[]{:S(2)}, u32[]{:S(2)}) collective-permute-start(bf16[16,1024]{1,0:T(8,128)(2,1)} %get-tuple-element.32), channel_id=1, source_target_pairs={{0,766},{1,767},{2,0},{3,1},{4,2},{5,3},{6,4},{7,5},{8,6},{9,7},{1... | collective-permute-start | bytes 98312 | tf_op jit(solution)/shard_map/ppermute | solution.py:202
  107.8 0.6 copy-start.3
  107.8 0.6 copy-start.5
  107.8 0.6 copy-start.6
  107.8 0.6 copy-start.7
Sparse Core Ops, SparseCore 0:
  10.4 66.5 all-gather.1

commit v5 on v4

--- a/solution.py
+++ b/solution.py
@@ -66,7 +66,7 @@
 
 def edge_kernel(
     panels, nodes_in, halo_0, halo_1, halo_2, halo_3, edges_in, gain_in, send_row_in, recv_row_in, node_cot_in, edge_cot_in,
-    new_nodes, new_edges, grad_pre, own, out_0, out_1, out_2, out_3, grad_recv,
+    new_nodes, new_edges, grad_pre, own, out_0, out_1, out_2, out_3, part,
     w_send, w_recv, w_edge, w_out, table_rows, edges, gain, send_row, recv_row, node_cot, edge_cot,
     sems, small_sems,
 ):
@@ -118,29 +118,25 @@
     own[...] = grad_lookup[:node_count]
     for j, out in enumerate((out_0, out_1, out_2, out_3)):
         out[...] = grad_lookup[node_count + j * halo : node_count + (j + 1) * halo].astype(BF)
-    grad_recv[...] = dot(to_recv, grad_preact).astype(BF)
+    grad_recv = dot(to_recv, grad_preact).astype(BF)
+    part[...] = node_cot[...].astype(F32) + dot_rows(grad_recv, matrix(w_recv))
 
 
 def local_kernel(
-    panels, grad_pre_in, grad_recv_in, recv_row_in, node_cot_in, edge_cot_in, grad_edges, part,
-    w_edge, w_recv, grad_pre, grad_recv, recv_row, node_cot, edge_cot, sems, small_sems,
+    panels, grad_pre_in, recv_row_in, node_cot_in, edge_cot_in, grad_edges,
+    w_edge, grad_pre, recv_row, node_cot, edge_cot, sems, small_sems,
 ):
     small = loads(
-        ((grad_pre_in, grad_pre), (recv_row_in, recv_row), (node_cot_in, node_cot), (edge_cot_in, edge_cot),
-         (grad_recv_in, grad_recv)),
-        small_sems,
-    )
-    copies = [fetches(panels, w_edge, sems.at[0], EDGE), fetches(panels, w_recv, sems.at[1], RECEIVE)]
-    begin(copies[0])
+        ((recv_row_in, recv_row), (node_cot_in, node_cot), (edge_cot_in, edge_cot), (grad_pre_in, grad_pre)), small_sems
+    )
+    copies = fetches(panels, w_edge, sems.at[0], EDGE)
     begin(small)
-    begin(copies[1])
+    begin(copies)
     finish(small)
     to_recv = one_hot_t(recv_row[...], node_cot.shape[0])
     grad_total = edge_cot[...].astype(F32) + picked(to_recv, node_cot[...])
-    finish(copies[0])
+    finish(copies)
     grad_edges[...] = (grad_total + dot_rows(grad_pre[...], matrix(w_edge))).astype(BF)
-    finish(copies[1])
-    part[...] = node_cot[...].astype(F32) + dot_rows(grad_recv[...], matrix(w_recv))
 
 
 def node_kernel(
@@ -215,9 +211,9 @@
     arrived = [moved(chosen[j], shifts[j]) for j in range(2 * spread)]
     gain = norm_gain.reshape(1, -1)
     send_row, recv_row = senders.reshape(1, -1), receivers.reshape(1, -1)
-    new_nodes, new_edges, grad_pre, own, *outgoing, grad_recv = run(
+    new_nodes, new_edges, grad_pre, own, *outgoing, part = run(
         edge_kernel,
-        (rows(nodes), rows(edges), rows(edges), rows(nodes, F32), *halo_rows, rows(nodes)),
+        (rows(nodes), rows(edges), rows(edges), rows(nodes, F32), *halo_rows, rows(nodes, F32)),
         4,
         2 * 768 * width * width,
         panels,
@@ -226,10 +222,8 @@
     )
     order = sorted(range(2 * spread), key=lambda j: (shifts[j] > 0, shifts[j]))
     back = [moved(outgoing[j], -shifts[j]) for j in order]
-    near = [grad_pre, grad_recv, recv_row, node_cotangent, edge_cotangent]
-    grad_edges, part = run(
-        local_kernel, (rows(edges), rows(nodes, F32)), 2, 2 * 256 * width * width, panels, near, near
-    )
+    near = [grad_pre, recv_row, node_cotangent, edge_cotangent]
+    grad_edges = run(local_kernel, rows(edges), 1, 2 * 192 * width * width, panels, near, near)
     last = [own, part, rows_by_shift, *back]
     grad_nodes = run(
         functools.partial(node_kernel, order), rows(nodes), 1, 2 * 64 * width * width, panels, last, last

time: 119 us -> 119 us (level)
  transfers between devices with their start and end apart: 9 -> 9, of which waited for: 2 -> 2; matrix products, arithmetic and copies ran while one was open for 0% -> 0% of each run, Pallas kernels for 6% -> 4%
where the time goes in v5:
time: 119 us; the launch traced here: 118 us
  starting transfers between devices  44.2 us (37%)
  waiting for transfers between devices  39.7 us (33%)
  Pallas kernels  17.4 us (15%)
  between operations  14.2 us (12%)
  other arithmetic  1.99 us (2%)
    ppermute x8, starting transfers between devices, moved(): lax.ppermute(value, AXES, [(i, (i + steps) % blocks) for i in range(block...  44.2 us
    all_gather x1, waiting for transfers between devices, shards(): lax.all_gather(mine.reshape(4 * panel, -1), ('core', 'mp'), axis=0, tiled...  37.8 us
    pallas_call x3, Pallas kernels, run(): pl.pallas_call(kernel, out_shape=outs, in_specs=[HBM] * (1 + len(values))...  15.6 us
  transfers between devices with their start and end apart: 9, of which 2 were waited for; matrix products, arithmetic and copies ran while one was open for 0% of the time, Pallas kernels for 4%

profile of v5, /device:TPU:8, one launch (start us, length us, event | category | flops | bytes accessed | tf_op | source)
XLA Modules:
  0.0 118.2 jit_solution(16954747777395554438)
XLA Ops:
  7.2 0.0 all-gather.2.cloned.1.call-start
  7.2 2.0 %fusion.2 = bf16[4,64,1024]{2,1,0:T(8,128)(2,1)} fusion(s32[]{:T(128)S(6)} %select_n.3, bf16[1,128,1024]{2,1,0:T(8,128)(2,1)} %bitcast.14, bf16[1,128,1024]{2,1,0:T(8,128)(2,1)} %bitcast.15, bf16[1,128,1024]{2,1,0:T(8,128)(2,1)} %bitcast.16, bf16[1,128,1024]{2,1,0:T(8,128)(2,1)} %bitcast.17), kind=kLoop, calls=%fused_computation.6 | loop fusion | flops 2097152 | bytes 1572868 | tf_op jit(solution)/shard_map/stack | solution.py:200
  9.2 0.0 all-gather.2.cloned.1.call-update
  9.2 1.8 %shard_map.147 = (bf16[16,1024]{1,0:T(8,128)(2,1)}, bf16[16,1024]{1,0:T(8,128)(2,1)}, bf16[16,1024]{1,0:T(8,128)(2,1)}, bf16[16,1024]{1,0:T(8,128)(2,1)}) custom-call(bf16[64,1024]{1,0:T(8,128)(2,1)} %nodes_in.1, s32[4,16]{1,0:T(4,128)} %bitcast.18), custom_call_target="tpu_custom_call" | custom-call | tf_op jit(solution)/shard_map/pallas_call | solution.py:210
  11.0 3.5 %collective-permute-start = (bf16[16,1024]{1,0:T(8,128)(2,1)}, bf16[16,1024]{1,0:T(8,128)(2,1)S(1)}, u32[]{:S(2)}, u32[]{:S(2)}) collective-permute-start(bf16[16,1024]{1,0:T(8,128)(2,1)} %get-tuple-element.17), channel_id=1, source_target_pairs={{0,1},{1,2},{2,3},{3,4},{4,5},{5,6},{6,7},{7,8},{8,9},{9,10},{10,1... | collective-permute-start | bytes 98312 | tf_op jit(solution)/shard_map/ppermute | solution.py:198
  14.5 5.7 %collective-permute-start.1 = (bf16[16,1024]{1,0:T(8,128)(2,1)}, bf16[16,1024]{1,0:T(8,128)(2,1)S(1)}, u32[]{:S(2)}, u32[]{:S(2)}) collective-permute-start(bf16[16,1024]{1,0:T(8,128)(2,1)} %get-tuple-element.18), channel_id=1, source_target_pairs={{0,2},{1,3},{2,4},{3,5},{4,6},{5,7},{6,8},{7,9},{8,10},{9,11},{10,... | collective-permute-start | bytes 98312 | tf_op jit(solution)/shard_map/ppermute | solution.py:198
  20.2 6.0 %collective-permute-start.2 = (bf16[16,1024]{1,0:T(8,128)(2,1)}, bf16[16,1024]{1,0:T(8,128)(2,1)S(1)}, u32[]{:S(2)}, u32[]{:S(2)}) collective-permute-start(bf16[16,1024]{1,0:T(8,128)(2,1)} %get-tuple-element.19), channel_id=1, source_target_pairs={{0,767},{1,0},{2,1},{3,2},{4,3},{5,4},{6,5},{7,6},{8,7},{9,8},{10,... | collective-permute-start | bytes 98312 | tf_op jit(solution)/shard_map/ppermute | solution.py:198
  26.2 11.0 %collective-permute-start.3 = (bf16[16,1024]{1,0:T(8,128)(2,1)}, bf16[16,1024]{1,0:T(8,128)(2,1)S(1)}, u32[]{:S(2)}, u32[]{:S(2)}) collective-permute-start(bf16[16,1024]{1,0:T(8,128)(2,1)} %get-tuple-element.20), channel_id=1, source_target_pairs={{0,766},{1,767},{2,0},{3,1},{4,2},{5,3},{6,4},{7,5},{8,6},{9,7},{1... | collective-permute-start | bytes 98312 | tf_op jit(solution)/shard_map/ppermute | solution.py:198
  37.2 0.0 collective-permute-done.halo_0
  37.2 0.0 copy-start
  37.3 0.0 copy-start.2
  37.3 1.8 %collective-permute-done.3.halo_3 = bf16[16,1024]{1,0:T(8,128)(2,1)S(1)} collective-permute-done((bf16[16,1024]{1,0:T(8,128)(2,1)}, bf16[16,1024]{1,0:T(8,128)(2,1)S(1)}, u32[]{:S(2)}, u32[]{:S(2)}) %collective-permute-start.3) | collective-permute-done | bytes 32800 | tf_op jit(solution)/shard_map/ppermute | solution.py:198
  39.1 37.8 %all-gather.2.cloned.1.call-done = bf16[4096,1024]{1,0:T(8,128)(2,1)} async-done(((bf16[256,1024]{1,0:T(8,128)(2,1)}), bf16[4096,1024]{1,0:T(8,128)(2,1)}) %all-gather.2.cloned.1.call-update) | async-done | bytes 8388624 | tf_op jit(solution)/shard_map/all_gather | solution.py:202
  77.0 8.6 %shard_map.148 = (bf16[64,1024]{1,0:T(8,128)(2,1)}, bf16[192,1024]{1,0:T(8,128)(2,1)}, bf16[192,1024]{1,0:T(8,128)(2,1)}, f32[64,1024]{1,0:T(8,128)}, bf16[16,10...) custom-call(bf16[2,8,4,64,1024]{4,3,2,1,0:T(8,128)(2,1)} %bitcast.10, ...), custom_call_target="tpu_custom_call" | custom-call | flops 1610612736 | bytes 4194304 | tf_op jit(solution)/shard_map/pallas_call | solution.py:161
  85.6 5.2 %collective-permute-start.4 = (bf16[16,1024]{1,0:T(8,128)(2,1)}, bf16[16,1024]{1,0:T(8,128)(2,1)S(1)}, u32[]{:S(2)}, u32[]{:S(2)}) collective-permute-start(bf16[16,1024]{1,0:T(8,128)(2,1)} %get-tuple-element.25), channel_id=1, source_target_pairs={{0,2},{1,3},{2,4},{3,5},{4,6},{5,7},{6,8},{7,9},{8,10},{9,11},{10,... | collective-permute-start | bytes 98312 | tf_op jit(solution)/shard_map/ppermute | solution.py:198
  90.8 2.5 %collective-permute-start.5 = (bf16[16,1024]{1,0:T(8,128)(2,1)}, bf16[16,1024]{1,0:T(8,128)(2,1)S(1)}, u32[]{:S(2)}, u32[]{:S(2)}) collective-permute-start(bf16[16,1024]{1,0:T(8,128)(2,1)} %get-tuple-element.26), channel_id=1, source_target_pairs={{0,1},{1,2},{2,3},{3,4},{4,5},{5,6},{6,7},{7,8},{8,9},{9,10},{10,1... | collective-permute-start | bytes 98312 | tf_op jit(solution)/shard_map/ppermute | solution.py:198
  93.3 3.3 %collective-permute-start.6 = (bf16[16,1024]{1,0:T(8,128)(2,1)}, bf16[16,1024]{1,0:T(8,128)(2,1)S(1)}, u32[]{:S(2)}, u32[]{:S(2)}) collective-permute-start(bf16[16,1024]{1,0:T(8,128)(2,1)} %get-tuple-element.27), channel_id=1, source_target_pairs={{0,767},{1,0},{2,1},{3,2},{4,3},{5,4},{6,5},{7,6},{8,7},{9,8},{10,... | collective-permute-start | bytes 98312 | tf_op jit(solution)/shard_map/ppermute | solution.py:198
  96.6 7.0 %collective-permute-start.7 = (bf16[16,1024]{1,0:T(8,128)(2,1)}, bf16[16,1024]{1,0:T(8,128)(2,1)S(1)}, u32[]{:S(2)}, u32[]{:S(2)}) collective-permute-start(bf16[16,1024]{1,0:T(8,128)(2,1)} %get-tuple-element.28), channel_id=1, source_target_pairs={{0,766},{1,767},{2,0},{3,1},{4,2},{5,3},{6,4},{7,5},{8,6},{9,7},{1... | collective-permute-start | bytes 98312 | tf_op jit(solution)/shard_map/ppermute | solution.py:198
  103.6 3.5 %shard_map.150 = bf16[192,1024]{1,0:T(8,128)(2,1)} custom-call(bf16[2,8,4,64,1024]{4,3,2,1,0:T(8,128)(2,1)} %bitcast.11, bf16[192,1024]{1,0:T(8,128)(2,1)} %get-tuple-element.29.grad_pre_in, s32[1,192]{1,0:T(1,128)} %bitcast.22, bf16[64,1024]{1,0:T(8,128)(2,1)} %node_cot_in.3, bf16[192,1024]{1,0:T(8,128)(2,1)} %edge_cot_in.3), custom_call_target="tpu_custom_call" | custom-call | flops 402653184 | bytes 4194304 | tf_op jit(solution)/shard_map/pallas_call | solution.py:161
  107.2 0.5 copy-done.3
  107.8 0.0 copy-done.5
  107.8 0.0 copy-done.6
  107.8 0.0 copy-done.7
  107.8 3.5 %shard_map.149 = bf16[64,1024]{1,0:T(8,128)(2,1)} custom-call(bf16[2,8,4,64,1024]{4,3,2,1,0:T(8,128)(2,1)} %bitcast.12, f32[64,1024]{1,0:T(8,128)} %get-tuple-element.23.own_in, f32[64,1024]{1,0:T(8,128)} %get-tuple-element.24.part_in, s32[4,16]{1,0:T(4,128)} %bitcast.19, bf16[16,1024]{1,0:T(8,128)(2,1)} %copy-done.3, bf16[16,1024]{1,0:T(8,128)(2,1)} %copy-done.5, ...), custom_call_target="tpu_custom_call" | custom-call | flops 134217728 | bytes 4194304 | tf_op jit(solution)/shard_map/pallas_call | solution.py:161
  (16 shorter events, 0.0 us)
Async XLA Ops:
  7.2 69.8 %all-gather.2.cloned.1.call-start = ((), (), s32[]{:S(2)}) async-start(), calls=%async_computation | async-start | bytes 8912896 | tf_op jit(solution)/shard_map/all_gather | solution.py:202
  11.0 26.2 %collective-permute-start = (bf16[16,1024]{1,0:T(8,128)(2,1)}, bf16[16,1024]{1,0:T(8,128)(2,1)S(1)}, u32[]{:S(2)}, u32[]{:S(2)}) collective-permute-start(bf16[16,1024]{1,0:T(8,128)(2,1)} %get-tuple-element.17), channel_id=1, source_target_pairs={{0,1},{1,2},{2,3},{3,4},{4,5},{5,6},{6,7},{7,8},{8,9},{9,10},{10,1... | collective-permute-start | bytes 98312 | tf_op jit(solution)/shard_map/ppermute | solution.py:198
  14.5 22.8 %collective-permute-start.1 = (bf16[16,1024]{1,0:T(8,128)(2,1)}, bf16[16,1024]{1,0:T(8,128)(2,1)S(1)}, u32[]{:S(2)}, u32[]{:S(2)}) collective-permute-start(bf16[16,1024]{1,0:T(8,128)(2,1)} %get-tuple-element.18), channel_id=1, source_target_pairs={{0,2},{1,3},{2,4},{3,5},{4,6},{5,7},{6,8},{7,9},{8,10},{9,11},{10,... | collective-permute-start | bytes 98312 | tf_op jit(solution)/shard_map/ppermute | solution.py:198
  20.2 17.1 %collective-permute-start.2 = (bf16[16,1024]{1,0:T(8,128)(2,1)}, bf16[16,1024]{1,0:T(8,128)(2,1)S(1)}, u32[]{:S(2)}, u32[]{:S(2)}) collective-permute-start(bf16[16,1024]{1,0:T(8,128)(2,1)} %get-tuple-element.19), channel_id=1, source_target_pairs={{0,767},{1,0},{2,1},{3,2},{4,3},{5,4},{6,5},{7,6},{8,7},{9,8},{10,... | collective-permute-start | bytes 98312 | tf_op jit(solution)/shard_map/ppermute | solution.py:198
  26.2 12.9 %collective-permute-start.3 = (bf16[16,1024]{1,0:T(8,128)(2,1)}, bf16[16,1024]{1,0:T(8,128)(2,1)S(1)}, u32[]{:S(2)}, u32[]{:S(2)}) collective-permute-start(bf16[16,1024]{1,0:T(8,128)(2,1)} %get-tuple-element.20), channel_id=1, source_target_pairs={{0,766},{1,767},{2,0},{3,1},{4,2},{5,3},{6,4},{7,5},{8,6},{9,7},{1... | collective-permute-start | bytes 98312 | tf_op jit(solution)/shard_map/ppermute | solution.py:198
  37.2 39.7 %copy-start = (bf16[16,1024]{1,0:T(8,128)(2,1)}, bf16[16,1024]{1,0:T(8,128)(2,1)S(1)}, u32[]{:S(2)}) copy-start(bf16[16,1024]{1,0:T(8,128)(2,1)S(1)} %collective-permute-done.halo_0) | copy-start | bytes 98308
  37.3 39.7 %copy-start.1 = (bf16[16,1024]{1,0:T(8,128)(2,1)}, bf16[16,1024]{1,0:T(8,128)(2,1)S(1)}, u32[]{:S(2)}) copy-start(bf16[16,1024]{1,0:T(8,128)(2,1)S(1)} %collective-permute-done.1.halo_1) | copy-start | bytes 98308
  37.3 39.7 %copy-start.2 = (bf16[16,1024]{1,0:T(8,128)(2,1)}, bf16[16,1024]{1,0:T(8,128)(2,1)S(1)}, u32[]{:S(2)}) copy-start(bf16[16,1024]{1,0:T(8,128)(2,1)S(1)} %collective-permute-done.2.halo_2) | copy-start | bytes 98308
  39.1 37.9 %copy-start.4 = (bf16[16,1024]{1,0:T(8,128)(2,1)}, bf16[16,1024]{1,0:T(8,128)(2,1)S(1)}, u32[]{:S(2)}) copy-start(bf16[16,1024]{1,0:T(8,128)(2,1)S(1)} %collective-permute-done.3.halo_3) | copy-start | bytes 98308
  85.6 21.5 %collective-permute-start.4 = (bf16[16,1024]{1,0:T(8,128)(2,1)}, bf16[16,1024]{1,0:T(8,128)(2,1)S(1)}, u32[]{:S(2)}, u32[]{:S(2)}) collective-permute-start(bf16[16,1024]{1,0:T(8,128)(2,1)} %get-tuple-element.25), channel_id=1, source_target_pairs={{0,2},{1,3},{2,4},{3,5},{4,6},{5,7},{6,8},{7,9},{8,10},{9,11},{10,... | collective-permute-start | bytes 98312 | tf_op jit(solution)/shard_map/ppermute | solution.py:198
  90.8 16.4 %collective-permute-start.5 = (bf16[16,1024]{1,0:T(8,128)(2,1)}, bf16[16,1024]{1,0:T(8,128)(2,1)S(1)}, u32[]{:S(2)}, u32[]{:S(2)}) collective-permute-start(bf16[16,1024]{1,0:T(8,128)(2,1)} %get-tuple-element.26), channel_id=1, source_target_pairs={{0,1},{1,2},{2,3},{3,4},{4,5},{5,6},{6,7},{7,8},{8,9},{9,10},{10,1... | collective-permute-start | bytes 98312 | tf_op jit(solution)/shard_map/ppermute | solution.py:198
  93.3 13.9 %collective-permute-start.6 = (bf16[16,1024]{1,0:T(8,128)(2,1)}, bf16[16,1024]{1,0:T(8,128)(2,1)S(1)}, u32[]{:S(2)}, u32[]{:S(2)}) collective-permute-start(bf16[16,1024]{1,0:T(8,128)(2,1)} %get-tuple-element.27), channel_id=1, source_target_pairs={{0,767},{1,0},{2,1},{3,2},{4,3},{5,4},{6,5},{7,6},{8,7},{9,8},{10,... | collective-permute-start | bytes 98312 | tf_op jit(solution)/shard_map/ppermute | solution.py:198
  96.6 10.6 %collective-permute-start.7 = (bf16[16,1024]{1,0:T(8,128)(2,1)}, bf16[16,1024]{1,0:T(8,128)(2,1)S(1)}, u32[]{:S(2)}, u32[]{:S(2)}) collective-permute-start(bf16[16,1024]{1,0:T(8,128)(2,1)} %get-tuple-element.28), channel_id=1, source_target_pairs={{0,766},{1,767},{2,0},{3,1},{4,2},{5,3},{6,4},{7,5},{8,6},{9,7},{1... | collective-permute-start | bytes 98312 | tf_op jit(solution)/shard_map/ppermute | solution.py:198
  107.1 0.6 copy-start.3
  107.2 0.6 copy-start.5
  107.2 0.6 copy-start.6
  107.2 0.6 copy-start.7
Sparse Core Ops, SparseCore 0:
  10.4 66.5 all-gather.1
